TPU v7x, 512 devices: a whole 4x8x8 slice. The times are simulated.
512 devices in a mesh: ctx: 64 (over y, z), head: 8 (over x, core).
Axes of the slice: x: 4, y: 8, z: 8, core: 2. Of those that a mesh axis runs over, the one named last changes fastest.
Arguments:
- queries: bfloat16 [32768, 6144], P(('ctx', 'head')), may hold values from -7 to 7
- keys: bfloat16 [32768, 1024], P(('ctx', 'head')), may hold values from -7 to 7
- values: bfloat16 [32768, 1024], P(('ctx', 'head')), may hold values from -6 to 6
- outputs: bfloat16 [32768, 6144], P(('ctx', 'head')), may hold values from -3 to 3
- grad_out: bfloat16 [32768, 6144], P(('ctx', 'head')), may hold values from -6 to 6
- first_block: int32 [128], replicated, may hold values from 0 to 126, as said below
Outputs:
- grad_queries: bfloat16 [32768, 6144], P(('ctx', 'head'))
- grad_keys: bfloat16 [32768, 1024], P(('ctx', 'head'))
- grad_values: bfloat16 [32768, 1024], P(('ctx', 'head'))
Inputs may be any that keep to these rules, and one draw needn't show every extreme that they name: first_block[c] lies between max(0, c - 3) and c; for the last block it is 124, and for the block before it it is 126.
All inputs are finite; a program needn't handle non-finite values.
Results may differ from a plain program's by a relative error of at most 0.0085.
Values may be sent and summed in bfloat16 or wider, within the bound.
A program may use at most 128 MiB of HBM per device.

v0:
```python
import jax
import jax.numpy as jnp
from jax import lax
from jax.sharding import PartitionSpec as P

HEAD_DIM = 128
BLOCK = 256
LOCAL_BLOCKS = 2
REACH = 2


def shifted(block, axis, distance):
    devices = range(lax.axis_size(axis))
    route = [(i - distance, i) for i in devices if i - distance in devices]
    return lax.ppermute(block, axis, route)


def shortened(x):

    def short(part):
        return part.astype(jnp.bfloat16) if part.dtype == jnp.float32 else part

    return jax.tree.map(short, x)


def split_heads(matrix):
    return matrix.reshape(matrix.shape[0], -1, HEAD_DIM).transpose(1, 0, 2)


def join_heads(stacked):
    return stacked.transpose(1, 0, 2).reshape(stacked.shape[1], -1)


def per_head(stacked, repeats):
    return jnp.repeat(stacked, repeats, axis=0)


def group_total(stacked, groups):
    return jnp.sum(stacked.reshape(groups, -1, stacked.shape[1], stacked.shape[2]), axis=1)


def local(queries, keys, values, outputs, grad_out, first_block):
    scaling = HEAD_DIM ** (-0.5)
    q_local, k_local, v_local, o_local, g_local = (
        lax.all_to_all(queries, "head", split_axis=1, concat_axis=0, tiled=True),
        lax.all_to_all(keys, "head", split_axis=1, concat_axis=0, tiled=True),
        lax.all_to_all(values, "head", split_axis=1, concat_axis=0, tiled=True),
        lax.all_to_all(outputs, "head", split_axis=1, concat_axis=0, tiled=True),
        lax.all_to_all(grad_out, "head", split_axis=1, concat_axis=0, tiled=True),
    )
    row_count = q_local.shape[0]
    groups = k_local.shape[1] // HEAD_DIM
    head_count = q_local.shape[1] // HEAD_DIM
    per_group = head_count // groups
    position = lax.axis_index("ctx")
    correction = jnp.sum(
        (g_local.astype(jnp.float32) * o_local.astype(jnp.float32)).reshape(
            row_count, -1, HEAD_DIM
        ),
        axis=2,
    )
    collected = [(k_local, v_local)]
    travelling = (k_local, v_local)
    for distance in range(REACH):
        travelling = shifted((travelling[0], travelling[1]), "ctx", 1)
        collected.append(travelling)
    collected = collected[::-1]
    band_keys = jnp.concatenate([member[0] for member in collected], axis=0)
    band_values = jnp.concatenate([member[1] for member in collected], axis=0)
    key_span = band_keys.shape[0]
    own_blocks = position * LOCAL_BLOCKS + jnp.arange(row_count, dtype=jnp.int32) // BLOCK
    own_first = jnp.repeat(
        lax.dynamic_slice_in_dim(first_block, position * LOCAL_BLOCKS, LOCAL_BLOCKS),
        BLOCK,
        total_repeat_length=row_count,
    )
    band_blocks = (position - REACH) * LOCAL_BLOCKS + jnp.arange(key_span, dtype=jnp.int32) // BLOCK
    visible = (band_blocks[None, :] >= own_first[:, None]) & (
        band_blocks[None, :] <= own_blocks[:, None]
    )
    query_heads = split_heads(q_local)
    grad_heads = split_heads(g_local)
    corr_heads = correction.T

    def probabilities(query_part, key_part):
        scores = jnp.dot(query_part, key_part.T, preferred_element_type=jnp.float32) * scaling
        scores = jnp.where(visible, scores, -1e30)
        row_max = jnp.max(scores, axis=1, keepdims=True)
        weights = jnp.where(visible, jnp.exp(scores - row_max), 0.0)
        row_total = jnp.sum(weights, axis=1, keepdims=True)
        return (weights / row_total, row_max[:, 0] + jnp.log(row_total[:, 0]))

    def head_partials(head_item):
        query_part, grad_part, key_part, value_part, corr_part = head_item
        probs = probabilities(query_part, key_part)[0]
        grad_probs = jnp.dot(grad_part, value_part.T, preferred_element_type=jnp.float32)
        grad_scores = (probs * (grad_probs - corr_part[:, None])).astype(jnp.bfloat16)
        probs_low = probs.astype(jnp.bfloat16)
        grad_query = jnp.dot(grad_scores, key_part, preferred_element_type=jnp.float32) * scaling
        key_term = jnp.dot(grad_scores.T, query_part, preferred_element_type=jnp.float32) * scaling
        value_term = jnp.dot(probs_low.T, grad_part, preferred_element_type=jnp.float32)
        return (grad_query, key_term, value_term)

    stacked_query, stacked_key, stacked_value = lax.map(
        head_partials,
        (
            query_heads,
            grad_heads,
            per_head(split_heads(band_keys), per_group),
            per_head(split_heads(band_values), per_group),
            corr_heads,
        ),
    )
    grad_q = join_heads(stacked_query)
    key_terms = join_heads(group_total(stacked_key, groups))
    value_terms = join_heads(group_total(stacked_value, groups))
    own_start = REACH * row_count
    grad_k = key_terms[own_start:]
    grad_v = value_terms[own_start:]
    for distance in range(1, REACH + 1):
        start_row = (REACH - distance) * row_count
        arrived = shifted(
            (
                shortened(key_terms[start_row : start_row + row_count]),
                shortened(value_terms[start_row : start_row + row_count]),
            ),
            "ctx",
            -distance,
        )
        grad_k = grad_k + arrived[0]
        grad_v = grad_v + arrived[1]
    return (
        lax.all_to_all(
            grad_q.astype(jnp.bfloat16), "head", split_axis=0, concat_axis=1, tiled=True
        ),
        lax.all_to_all(
            grad_k.astype(jnp.bfloat16), "head", split_axis=0, concat_axis=1, tiled=True
        ),
        lax.all_to_all(
            grad_v.astype(jnp.bfloat16), "head", split_axis=0, concat_axis=1, tiled=True
        ),
    )


def solution(mesh):
    placed = (
        P(("ctx", "head"), None),
        P(("ctx", "head"), None),
        P(("ctx", "head"), None),
        P(("ctx", "head"), None),
        P(("ctx", "head"), None),
        P(),
    )
    return jax.shard_map(
        local,
        mesh=mesh,
        in_specs=placed,
        out_specs=(P(("ctx", "head"), None), P(("ctx", "head"), None), P(("ctx", "head"), None)),
        check_vma=False,
    )
```

profile of v0, /device:TPU:1, one launch (start us, length us, event | category | flops | bytes accessed | tf_op | source)
XLA Modules:
  0.0 218.8 jit_solution(4158534329585170258)
XLA Ops:
  2.2 10.2 %all-to-all-start.1 = ((bf16[64,8,128]{2,0,1:T(8,128)(2,1)}), bf16[64,8,128]{2,0,1:T(8,128)(2,1)S(1)}, u32[]{:S(2)}, u32[]{:S(2)}) async-start(bf16[64,8,128]{2,0,1:T(8,128)(2,1)} %copy_bitcast_fusion.6), calls=%async_computation.1 | async-start | bytes 262144 | tf_op jit(solution)/shard_map/all_to_all | solution.py:46
  14.0 3.7 %all-to-all-done.1 = bf16[64,8,128]{2,0,1:T(8,128)(2,1)S(1)} async-done(((bf16[64,8,128]{2,0,1:T(8,128)(2,1)}), bf16[64,8,128]{2,0,1:T(8,128)(2,1)S(1)}, u32[]{:S(2)}, u32[]{:S(2)}) %all-to-all-start.1) | async-done | bytes 131104 | tf_op jit(solution)/shard_map/all_to_all | solution.py:46
  17.7 4.1 %all-to-all-start.3 = ((bf16[64,8,128]{2,0,1:T(8,128)(2,1)}), bf16[64,8,128]{2,0,1:T(8,128)(2,1)S(1)}, u32[]{:S(2)}, u32[]{:S(2)}) async-start(bf16[64,8,128]{2,0,1:T(8,128)(2,1)} %copy_bitcast_fusion.5), calls=%async_computation.3 | async-start | bytes 262144 | tf_op jit(solution)/shard_map/all_to_all | solution.py:47
  21.8 2.1 copy.69
  24.0 3.1 %all-to-all-done.3 = bf16[64,8,128]{2,0,1:T(8,128)(2,1)S(1)} async-done(((bf16[64,8,128]{2,0,1:T(8,128)(2,1)}), bf16[64,8,128]{2,0,1:T(8,128)(2,1)S(1)}, u32[]{:S(2)}, u32[]{:S(2)}) %all-to-all-start.3) | async-done | bytes 131104 | tf_op jit(solution)/shard_map/all_to_all | solution.py:47
  27.1 4.3 %all-to-all-start = ((bf16[64,8,768]{2,0,1:T(8,128)(2,1)}), bf16[64,8,768]{2,0,1:T(8,128)(2,1)S(1)}, u32[]{:S(2)}, u32[]{:S(2)}) async-start(bf16[64,8,768]{2,0,1:T(8,128)(2,1)} %bitcast.121), calls=%async_computation | async-start | bytes 1572864 | tf_op jit(solution)/shard_map/all_to_all | solution.py:45
  32.4 11.4 %all-to-all-done = bf16[64,8,768]{2,0,1:T(8,128)(2,1)S(1)} async-done(((bf16[64,8,768]{2,0,1:T(8,128)(2,1)}), bf16[64,8,768]{2,0,1:T(8,128)(2,1)S(1)}, u32[]{:S(2)}, u32[]{:S(2)}) %all-to-all-start) | async-done | bytes 786464 | tf_op jit(solution)/shard_map/all_to_all | solution.py:45
  43.7 4.3 %all-to-all-start.4 = ((bf16[64,8,768]{2,0,1:T(8,128)(2,1)}), bf16[64,8,768]{2,0,1:T(8,128)(2,1)S(1)}, u32[]{:S(2)}, u32[]{:S(2)}) async-start(bf16[64,8,768]{2,0,1:T(8,128)(2,1)} %bitcast.119), calls=%async_computation.4 | async-start | bytes 1572864 | tf_op jit(solution)/shard_map/all_to_all | solution.py:48
  50.0 2.3 %collective-permute-start = (bf16[512,128]{1,0:T(8,128)(2,1)S(1)}, bf16[512,128]{1,0:T(8,128)(2,1)S(1)}, u32[]{:S(2)}, u32[]{:S(2)}) collective-permute-start(bf16[512,128]{1,0:T(8,128)(2,1)S(1)} %bitcast.160), channel_id=1, source_target_pairs={{0,8},{8,16},{16,24},{24,32},{32,40},{40,48},{48,56},{56,64},{64,7... | collective-permute-start | bytes 393224 | tf_op jit(solution)/shard_map/ppermute | solution.py:15
  52.4 4.1 %collective-permute-start.3 = (bf16[512,128]{1,0:T(8,128)(2,1)S(1)}, bf16[512,128]{1,0:T(8,128)(2,1)S(1)}, u32[]{:S(2)}, u32[]{:S(2)}) collective-permute-start(bf16[512,128]{1,0:T(8,128)(2,1)S(1)} %collective-permute-done.2), channel_id=1, source_target_pairs={{0,8},{8,16},{16,24},{24,32},{32,40},{40,48},{48,56},{56,64},{64,7... | collective-permute-start | bytes 393224 | tf_op jit(solution)/shard_map/ppermute | solution.py:15
  58.7 5.1 %collective-permute-start.1 = (bf16[512,128]{1,0:T(8,128)(2,1)S(1)}, bf16[512,128]{1,0:T(8,128)(2,1)S(1)}, u32[]{:S(2)}, u32[]{:S(2)}) collective-permute-start(bf16[512,128]{1,0:T(8,128)(2,1)S(1)} %collective-permute-done), channel_id=1, source_target_pairs={{0,8},{8,16},{16,24},{24,32},{32,40},{40,48},{48,56},{56,64},{64,7... | collective-permute-start | bytes 393224 | tf_op jit(solution)/shard_map/ppermute | solution.py:15
  63.9 6.0 %all-to-all-start.2 = ((bf16[64,8,768]{2,0,1:T(8,128)(2,1)}), bf16[64,8,768]{2,0,1:T(8,128)(2,1)}, u32[]{:S(2)}, u32[]{:S(2)}) async-start(bf16[64,8,768]{2,0,1:T(8,128)(2,1)} %bitcast.120), calls=%async_computation.2 | async-start | bytes 1572864 | tf_op jit(solution)/shard_map/all_to_all | solution.py:49
  76.0 6.2 %all-to-all-done.2 = bf16[64,8,768]{2,0,1:T(8,128)(2,1)} async-done(((bf16[64,8,768]{2,0,1:T(8,128)(2,1)}), bf16[64,8,768]{2,0,1:T(8,128)(2,1)}, u32[]{:S(2)}, u32[]{:S(2)}) %all-to-all-start.2) | async-done | bytes 786464 | tf_op jit(solution)/shard_map/all_to_all | solution.py:49
  82.2 2.0 reshape.182
  89.0 72.2 %while.16 = (s32[]{:T(128)}, bf16[6,512,128]{2,1,0:T(8,128)(2,1)}, f32[6,1536,128]{2,1,0:T(8,128)}, f32[6,1536,128]{2,1,0:T(8,128)}, bf16[6,512,128]{2,1,0:T(8,1...) while((s32[]{:T(128)}, bf16[6,512,128]{2,1,0:T(8,128)(2,1)}, ...), condition=%wide.region_4.5_spmd.clone, body=%wide.region_1.4_spmd.clone.sunk | while | flops 1028914176 | bytes 20909192 | solution.py:104
  89.0 1.9 fusion.77
  91.9 2.3 %fusion.79 = bf16[512,1536]{1,0:T(8,128)(2,1)S(1)} fusion(f32[512]{0:T(512)S(1)} %bitcast.164, bf16[6,1536,128]{2,1,0:T(8,128)(2,1)} %get-tuple-element.293, s32[]{:T(128)S(6)} %copy.77, bf16[6,512,128]{2,1,0:T(8,128)(2,1)} %get-tuple-element.292, f32[512]{0:T(512)S(1)} %fusion.78, f32[512,1536]{1,0:T(8,128)S(1)} %get-tuple-element.258, ...), kind=kOutput, calls=%fused_computation.7.clone.1 | convolution fusion | flops 208404480 | bytes 5260288 | tf_op jit(solution)/shard_map/while/body/eval_jaxpr/dot_general | solution.py:96
  95.4 3.2 %fusion.82 = f32[6,1536,128]{2,1,0:T(8,128)} fusion(f32[6,1536,128]{2,1,0:T(8,128)} %get-tuple-element.276, s32[]{:T(128)S(6)} %copy.77, bf16[6,512,128]{2,1,0:T(8,128)(2,1)} %get-tuple-element.292, f32[512,1536]{1,0:T(8,128)S(1)} %get-tuple-element.258, s32[1536]{0:T(1024)S(1)} %get-tuple-element.297, f32[512]{0:T(512)S(1)} %fusion.78, ...), kind=kOutput, calls=%fused_computation.10.clone.1 | convolution fusion | flops 206831616 | bytes 4078592 | tf_op jit(solution)/shard_map/while/body/eval_jaxpr/dot_general | solution.py:101
  98.6 2.4 %fusion.81 = f32[6,1536,128]{2,1,0:T(8,128)} fusion(f32[6,1536,128]{2,1,0:T(8,128)} %get-tuple-element.275, s32[]{:T(128)S(6)} %copy.77, bf16[512,1536]{1,0:T(8,128)(2,1)S(1)} %fusion.79, bf16[6,512,128]{2,1,0:T(8,128)(2,1)} %get-tuple-element.290), kind=kOutput, calls=%fused_computation.12.clone.1 | convolution fusion | flops 201523200 | bytes 2491392 | tf_op jit(solution)/shard_map/while/body/eval_jaxpr/dot_general | solution.py:100
  101.0 1.9 fusion.77
  103.9 2.3 %fusion.79 = bf16[512,1536]{1,0:T(8,128)(2,1)S(1)} fusion(f32[512]{0:T(512)S(1)} %bitcast.164, bf16[6,1536,128]{2,1,0:T(8,128)(2,1)} %get-tuple-element.293, s32[]{:T(128)S(6)} %copy.77, bf16[6,512,128]{2,1,0:T(8,128)(2,1)} %get-tuple-element.292, f32[512]{0:T(512)S(1)} %fusion.78, f32[512,1536]{1,0:T(8,128)S(1)} %get-tuple-element.258, ...), kind=kOutput, calls=%fused_computation.7.clone.1 | convolution fusion | flops 208404480 | bytes 5260288 | tf_op jit(solution)/shard_map/while/body/eval_jaxpr/dot_general | solution.py:96
  107.5 3.2 %fusion.82 = f32[6,1536,128]{2,1,0:T(8,128)} fusion(f32[6,1536,128]{2,1,0:T(8,128)} %get-tuple-element.276, s32[]{:T(128)S(6)} %copy.77, bf16[6,512,128]{2,1,0:T(8,128)(2,1)} %get-tuple-element.292, f32[512,1536]{1,0:T(8,128)S(1)} %get-tuple-element.258, s32[1536]{0:T(1024)S(1)} %get-tuple-element.297, f32[512]{0:T(512)S(1)} %fusion.78, ...), kind=kOutput, calls=%fused_computation.10.clone.1 | convolution fusion | flops 206831616 | bytes 4078592 | tf_op jit(solution)/shard_map/while/body/eval_jaxpr/dot_general | solution.py:101
  110.6 2.4 %fusion.81 = f32[6,1536,128]{2,1,0:T(8,128)} fusion(f32[6,1536,128]{2,1,0:T(8,128)} %get-tuple-element.275, s32[]{:T(128)S(6)} %copy.77, bf16[512,1536]{1,0:T(8,128)(2,1)S(1)} %fusion.79, bf16[6,512,128]{2,1,0:T(8,128)(2,1)} %get-tuple-element.290), kind=kOutput, calls=%fused_computation.12.clone.1 | convolution fusion | flops 201523200 | bytes 2491392 | tf_op jit(solution)/shard_map/while/body/eval_jaxpr/dot_general | solution.py:100
  113.1 1.9 fusion.77
  115.9 2.3 %fusion.79 = bf16[512,1536]{1,0:T(8,128)(2,1)S(1)} fusion(f32[512]{0:T(512)S(1)} %bitcast.164, bf16[6,1536,128]{2,1,0:T(8,128)(2,1)} %get-tuple-element.293, s32[]{:T(128)S(6)} %copy.77, bf16[6,512,128]{2,1,0:T(8,128)(2,1)} %get-tuple-element.292, f32[512]{0:T(512)S(1)} %fusion.78, f32[512,1536]{1,0:T(8,128)S(1)} %get-tuple-element.258, ...), kind=kOutput, calls=%fused_computation.7.clone.1 | convolution fusion | flops 208404480 | bytes 5260288 | tf_op jit(solution)/shard_map/while/body/eval_jaxpr/dot_general | solution.py:96
  119.5 3.2 %fusion.82 = f32[6,1536,128]{2,1,0:T(8,128)} fusion(f32[6,1536,128]{2,1,0:T(8,128)} %get-tuple-element.276, s32[]{:T(128)S(6)} %copy.77, bf16[6,512,128]{2,1,0:T(8,128)(2,1)} %get-tuple-element.292, f32[512,1536]{1,0:T(8,128)S(1)} %get-tuple-element.258, s32[1536]{0:T(1024)S(1)} %get-tuple-element.297, f32[512]{0:T(512)S(1)} %fusion.78, ...), kind=kOutput, calls=%fused_computation.10.clone.1 | convolution fusion | flops 206831616 | bytes 4078592 | tf_op jit(solution)/shard_map/while/body/eval_jaxpr/dot_general | solution.py:101
  122.7 2.4 %fusion.81 = f32[6,1536,128]{2,1,0:T(8,128)} fusion(f32[6,1536,128]{2,1,0:T(8,128)} %get-tuple-element.275, s32[]{:T(128)S(6)} %copy.77, bf16[512,1536]{1,0:T(8,128)(2,1)S(1)} %fusion.79, bf16[6,512,128]{2,1,0:T(8,128)(2,1)} %get-tuple-element.290), kind=kOutput, calls=%fused_computation.12.clone.1 | convolution fusion | flops 201523200 | bytes 2491392 | tf_op jit(solution)/shard_map/while/body/eval_jaxpr/dot_general | solution.py:100
  125.1 1.9 fusion.77
  127.9 2.3 %fusion.79 = bf16[512,1536]{1,0:T(8,128)(2,1)S(1)} fusion(f32[512]{0:T(512)S(1)} %bitcast.164, bf16[6,1536,128]{2,1,0:T(8,128)(2,1)} %get-tuple-element.293, s32[]{:T(128)S(6)} %copy.77, bf16[6,512,128]{2,1,0:T(8,128)(2,1)} %get-tuple-element.292, f32[512]{0:T(512)S(1)} %fusion.78, f32[512,1536]{1,0:T(8,128)S(1)} %get-tuple-element.258, ...), kind=kOutput, calls=%fused_computation.7.clone.1 | convolution fusion | flops 208404480 | bytes 5260288 | tf_op jit(solution)/shard_map/while/body/eval_jaxpr/dot_general | solution.py:96
  131.5 3.2 %fusion.82 = f32[6,1536,128]{2,1,0:T(8,128)} fusion(f32[6,1536,128]{2,1,0:T(8,128)} %get-tuple-element.276, s32[]{:T(128)S(6)} %copy.77, bf16[6,512,128]{2,1,0:T(8,128)(2,1)} %get-tuple-element.292, f32[512,1536]{1,0:T(8,128)S(1)} %get-tuple-element.258, s32[1536]{0:T(1024)S(1)} %get-tuple-element.297, f32[512]{0:T(512)S(1)} %fusion.78, ...), kind=kOutput, calls=%fused_computation.10.clone.1 | convolution fusion | flops 206831616 | bytes 4078592 | tf_op jit(solution)/shard_map/while/body/eval_jaxpr/dot_general | solution.py:101
  134.7 2.4 %fusion.81 = f32[6,1536,128]{2,1,0:T(8,128)} fusion(f32[6,1536,128]{2,1,0:T(8,128)} %get-tuple-element.275, s32[]{:T(128)S(6)} %copy.77, bf16[512,1536]{1,0:T(8,128)(2,1)S(1)} %fusion.79, bf16[6,512,128]{2,1,0:T(8,128)(2,1)} %get-tuple-element.290), kind=kOutput, calls=%fused_computation.12.clone.1 | convolution fusion | flops 201523200 | bytes 2491392 | tf_op jit(solution)/shard_map/while/body/eval_jaxpr/dot_general | solution.py:100
  137.1 1.9 fusion.77
  140.0 2.3 %fusion.79 = bf16[512,1536]{1,0:T(8,128)(2,1)S(1)} fusion(f32[512]{0:T(512)S(1)} %bitcast.164, bf16[6,1536,128]{2,1,0:T(8,128)(2,1)} %get-tuple-element.293, s32[]{:T(128)S(6)} %copy.77, bf16[6,512,128]{2,1,0:T(8,128)(2,1)} %get-tuple-element.292, f32[512]{0:T(512)S(1)} %fusion.78, f32[512,1536]{1,0:T(8,128)S(1)} %get-tuple-element.258, ...), kind=kOutput, calls=%fused_computation.7.clone.1 | convolution fusion | flops 208404480 | bytes 5260288 | tf_op jit(solution)/shard_map/while/body/eval_jaxpr/dot_general | solution.py:96
  143.5 3.2 %fusion.82 = f32[6,1536,128]{2,1,0:T(8,128)} fusion(f32[6,1536,128]{2,1,0:T(8,128)} %get-tuple-element.276, s32[]{:T(128)S(6)} %copy.77, bf16[6,512,128]{2,1,0:T(8,128)(2,1)} %get-tuple-element.292, f32[512,1536]{1,0:T(8,128)S(1)} %get-tuple-element.258, s32[1536]{0:T(1024)S(1)} %get-tuple-element.297, f32[512]{0:T(512)S(1)} %fusion.78, ...), kind=kOutput, calls=%fused_computation.10.clone.1 | convolution fusion | flops 206831616 | bytes 4078592 | tf_op jit(solution)/shard_map/while/body/eval_jaxpr/dot_general | solution.py:101
  146.8 2.4 %fusion.81 = f32[6,1536,128]{2,1,0:T(8,128)} fusion(f32[6,1536,128]{2,1,0:T(8,128)} %get-tuple-element.275, s32[]{:T(128)S(6)} %copy.77, bf16[512,1536]{1,0:T(8,128)(2,1)S(1)} %fusion.79, bf16[6,512,128]{2,1,0:T(8,128)(2,1)} %get-tuple-element.290), kind=kOutput, calls=%fused_computation.12.clone.1 | convolution fusion | flops 201523200 | bytes 2491392 | tf_op jit(solution)/shard_map/while/body/eval_jaxpr/dot_general | solution.py:100
  149.2 1.9 fusion.77
  152.0 2.3 %fusion.79 = bf16[512,1536]{1,0:T(8,128)(2,1)S(1)} fusion(f32[512]{0:T(512)S(1)} %bitcast.164, bf16[6,1536,128]{2,1,0:T(8,128)(2,1)} %get-tuple-element.293, s32[]{:T(128)S(6)} %copy.77, bf16[6,512,128]{2,1,0:T(8,128)(2,1)} %get-tuple-element.292, f32[512]{0:T(512)S(1)} %fusion.78, f32[512,1536]{1,0:T(8,128)S(1)} %get-tuple-element.258, ...), kind=kOutput, calls=%fused_computation.7.clone.1 | convolution fusion | flops 208404480 | bytes 5260288 | tf_op jit(solution)/shard_map/while/body/eval_jaxpr/dot_general | solution.py:96
  155.6 3.2 %fusion.82 = f32[6,1536,128]{2,1,0:T(8,128)} fusion(f32[6,1536,128]{2,1,0:T(8,128)} %get-tuple-element.276, s32[]{:T(128)S(6)} %copy.77, bf16[6,512,128]{2,1,0:T(8,128)(2,1)} %get-tuple-element.292, f32[512,1536]{1,0:T(8,128)S(1)} %get-tuple-element.258, s32[1536]{0:T(1024)S(1)} %get-tuple-element.297, f32[512]{0:T(512)S(1)} %fusion.78, ...), kind=kOutput, calls=%fused_computation.10.clone.1 | convolution fusion | flops 206831616 | bytes 4078592 | tf_op jit(solution)/shard_map/while/body/eval_jaxpr/dot_general | solution.py:101
  158.8 2.4 %fusion.81 = f32[6,1536,128]{2,1,0:T(8,128)} fusion(f32[6,1536,128]{2,1,0:T(8,128)} %get-tuple-element.275, s32[]{:T(128)S(6)} %copy.77, bf16[512,1536]{1,0:T(8,128)(2,1)S(1)} %fusion.79, bf16[6,512,128]{2,1,0:T(8,128)(2,1)} %get-tuple-element.290), kind=kOutput, calls=%fused_computation.12.clone.1 | convolution fusion | flops 201523200 | bytes 2491392 | tf_op jit(solution)/shard_map/while/body/eval_jaxpr/dot_general | solution.py:100
  161.2 2.7 %reduce_sum.43 = f32[1536,128]{1,0:T(8,128)S(1)} reduce(f32[6,1536,128]{2,1,0:T(8,128)} %get-tuple-element.71, f32[]{:T(128)} %constant.160.clone.1), dimensions={0}, to_apply=%region_6.7 | reduce | flops 983040 | bytes 5505028 | tf_op jit(solution)/shard_map/reduce_sum | solution.py:39
  163.9 2.7 %reduce_sum.41 = f32[1536,128]{1,0:T(8,128)S(1)} reduce(f32[6,1536,128]{2,1,0:T(8,128)} %get-tuple-element.70, f32[]{:T(128)} %constant.160.clone.1), dimensions={0}, to_apply=%region_5.6 | reduce | flops 983040 | bytes 5505028 | tf_op jit(solution)/shard_map/reduce_sum | solution.py:39
  172.8 6.5 %collective-permute-done.5 = bf16[512,128]{1,0:T(8,128)(2,1)S(1)} collective-permute-done((bf16[512,128]{1,0:T(8,128)(2,1)S(1)}, bf16[512,128]{1,0:T(8,128)(2,1)S(1)}, u32[]{:S(2)}, u32[]{:S(2)}) %collective-permute-start.5) | collective-permute-done | bytes 131104 | tf_op jit(solution)/shard_map/ppermute | solution.py:15
  180.0 6.5 %all-to-all-start.6 = ((bf16[8,64,128]{2,1,0:T(8,128)(2,1)}), bf16[8,64,128]{2,1,0:T(8,128)(2,1)S(1)}, u32[]{:S(2)}, u32[]{:S(2)}) async-start(bf16[8,64,128]{2,1,0:T(8,128)(2,1)} %bitcast.18), calls=%async_computation.6 | async-start | bytes 262144 | tf_op jit(solution)/shard_map/all_to_all | solution.py:136
  188.6 3.2 %all-to-all-done.6 = bf16[8,64,128]{2,1,0:T(8,128)(2,1)S(1)} async-done(((bf16[8,64,128]{2,1,0:T(8,128)(2,1)}), bf16[8,64,128]{2,1,0:T(8,128)(2,1)S(1)}, u32[]{:S(2)}, u32[]{:S(2)}) %all-to-all-start.6) | async-done | bytes 131104 | tf_op jit(solution)/shard_map/all_to_all | solution.py:136
  191.8 4.1 %all-to-all-start.7 = ((bf16[8,64,128]{2,1,0:T(8,128)(2,1)}), bf16[8,64,128]{2,1,0:T(8,128)(2,1)S(1)}, u32[]{:S(2)}, u32[]{:S(2)}) async-start(bf16[8,64,128]{2,1,0:T(8,128)(2,1)} %bitcast.24), calls=%async_computation.7 | async-start | bytes 262144 | tf_op jit(solution)/shard_map/all_to_all | solution.py:139
  198.3 3.0 %all-to-all-done.7 = bf16[8,64,128]{2,1,0:T(8,128)(2,1)S(1)} async-done(((bf16[8,64,128]{2,1,0:T(8,128)(2,1)}), bf16[8,64,128]{2,1,0:T(8,128)(2,1)S(1)}, u32[]{:S(2)}, u32[]{:S(2)}) %all-to-all-start.7) | async-done | bytes 131104 | tf_op jit(solution)/shard_map/all_to_all | solution.py:139
  201.3 4.3 %all-to-all-start.5 = ((bf16[8,64,768]{2,1,0:T(8,128)(2,1)}), bf16[8,64,768]{2,1,0:T(8,128)(2,1)S(1)}, u32[]{:S(2)}, u32[]{:S(2)}) async-start(bf16[8,64,768]{2,1,0:T(8,128)(2,1)} %convert_element_type.70), calls=%async_computation.5 | async-start | bytes 1572864 | tf_op jit(solution)/shard_map/all_to_all | solution.py:133
  206.9 11.0 %all-to-all-done.5 = bf16[8,64,768]{2,1,0:T(8,128)(2,1)S(1)} async-done(((bf16[8,64,768]{2,1,0:T(8,128)(2,1)}), bf16[8,64,768]{2,1,0:T(8,128)(2,1)S(1)}, u32[]{:S(2)}, u32[]{:S(2)}) %all-to-all-start.5) | async-done | bytes 786464 | tf_op jit(solution)/shard_map/all_to_all | solution.py:133
  (78 shorter events, 46.2 us)
Async XLA Ops:
  0.6 0.9 copy-start
  0.6 30.8 %copy-start.3 = (bf16[64,6144]{1,0:T(8,128)(2,1)S(1)}, bf16[64,6144]{1,0:T(8,128)(2,1)}, u32[]{:S(2)}) copy-start(bf16[64,6144]{1,0:T(8,128)(2,1)} %param.13) | copy-start | bytes 2359300
  2.2 15.4 %all-to-all-start.1 = ((bf16[64,8,128]{2,0,1:T(8,128)(2,1)}), bf16[64,8,128]{2,0,1:T(8,128)(2,1)S(1)}, u32[]{:S(2)}, u32[]{:S(2)}) async-start(bf16[64,8,128]{2,0,1:T(8,128)(2,1)} %copy_bitcast_fusion.6), calls=%async_computation.1 | async-start | bytes 262144 | tf_op jit(solution)/shard_map/all_to_all | solution.py:46
  17.7 9.4 %all-to-all-start.3 = ((bf16[64,8,128]{2,0,1:T(8,128)(2,1)}), bf16[64,8,128]{2,0,1:T(8,128)(2,1)S(1)}, u32[]{:S(2)}, u32[]{:S(2)}) async-start(bf16[64,8,128]{2,0,1:T(8,128)(2,1)} %copy_bitcast_fusion.5), calls=%async_computation.3 | async-start | bytes 262144 | tf_op jit(solution)/shard_map/all_to_all | solution.py:47
  21.8 27.5 %copy-start.6 = (s32[128]{0:T(128)S(1)}, s32[128]{0:T(128)}, u32[]{:S(2)}) copy-start(s32[128]{0:T(128)} %param.15) | copy-start | bytes 1540
  21.8 34.6 %copy-start.5 = (pred[512]{0:T(512)(128)(4,1)S(1)}, pred[512]{0:T(512)(128)(4,1)}, u32[]{:S(2)}) copy-start(pred[512]{0:T(512)(128)(4,1)} %constant.179) | copy-start | bytes 1540
  21.8 36.0 %copy-start.4 = (bf16[64,6144]{1,0:T(8,128)(2,1)S(1)}, bf16[64,6144]{1,0:T(8,128)(2,1)}, u32[]{:S(2)}) copy-start(bf16[64,6144]{1,0:T(8,128)(2,1)} %param.14) | copy-start | bytes 2359300
  27.1 16.6 %all-to-all-start = ((bf16[64,8,768]{2,0,1:T(8,128)(2,1)}), bf16[64,8,768]{2,0,1:T(8,128)(2,1)S(1)}, u32[]{:S(2)}, u32[]{:S(2)}) async-start(bf16[64,8,768]{2,0,1:T(8,128)(2,1)} %bitcast.121), calls=%async_computation | async-start | bytes 1572864 | tf_op jit(solution)/shard_map/all_to_all | solution.py:45
  43.7 20.1 %all-to-all-start.4 = ((bf16[64,8,768]{2,0,1:T(8,128)(2,1)}), bf16[64,8,768]{2,0,1:T(8,128)(2,1)S(1)}, u32[]{:S(2)}, u32[]{:S(2)}) async-start(bf16[64,8,768]{2,0,1:T(8,128)(2,1)} %bitcast.119), calls=%async_computation.4 | async-start | bytes 1572864 | tf_op jit(solution)/shard_map/all_to_all | solution.py:48
  48.0 4.3 %collective-permute-start.2 = (bf16[512,128]{1,0:T(8,128)(2,1)S(1)}, bf16[512,128]{1,0:T(8,128)(2,1)S(1)}, u32[]{:S(2)}, u32[]{:S(2)}) collective-permute-start(bf16[512,128]{1,0:T(8,128)(2,1)S(1)} %bitcast.162), channel_id=1, source_target_pairs={{0,8},{8,16},{16,24},{24,32},{32,40},{40,48},{48,56},{56,64},{64,7... | collective-permute-start | bytes 393224 | tf_op jit(solution)/shard_map/ppermute | solution.py:15
  50.0 8.7 %collective-permute-start = (bf16[512,128]{1,0:T(8,128)(2,1)S(1)}, bf16[512,128]{1,0:T(8,128)(2,1)S(1)}, u32[]{:S(2)}, u32[]{:S(2)}) collective-permute-start(bf16[512,128]{1,0:T(8,128)(2,1)S(1)} %bitcast.160), channel_id=1, source_target_pairs={{0,8},{8,16},{16,24},{24,32},{32,40},{40,48},{48,56},{56,64},{64,7... | collective-permute-start | bytes 393224 | tf_op jit(solution)/shard_map/ppermute | solution.py:15
  52.4 17.5 %collective-permute-start.3 = (bf16[512,128]{1,0:T(8,128)(2,1)S(1)}, bf16[512,128]{1,0:T(8,128)(2,1)S(1)}, u32[]{:S(2)}, u32[]{:S(2)}) collective-permute-start(bf16[512,128]{1,0:T(8,128)(2,1)S(1)} %collective-permute-done.2), channel_id=1, source_target_pairs={{0,8},{8,16},{16,24},{24,32},{32,40},{40,48},{48,56},{56,64},{64,7... | collective-permute-start | bytes 393224 | tf_op jit(solution)/shard_map/ppermute | solution.py:15
  58.7 11.9 %collective-permute-start.1 = (bf16[512,128]{1,0:T(8,128)(2,1)S(1)}, bf16[512,128]{1,0:T(8,128)(2,1)S(1)}, u32[]{:S(2)}, u32[]{:S(2)}) collective-permute-start(bf16[512,128]{1,0:T(8,128)(2,1)S(1)} %collective-permute-done), channel_id=1, source_target_pairs={{0,8},{8,16},{16,24},{24,32},{32,40},{40,48},{48,56},{56,64},{64,7... | collective-permute-start | bytes 393224 | tf_op jit(solution)/shard_map/ppermute | solution.py:15
  63.9 18.4 %all-to-all-start.2 = ((bf16[64,8,768]{2,0,1:T(8,128)(2,1)}), bf16[64,8,768]{2,0,1:T(8,128)(2,1)}, u32[]{:S(2)}, u32[]{:S(2)}) async-start(bf16[64,8,768]{2,0,1:T(8,128)(2,1)} %bitcast.120), calls=%async_computation.2 | async-start | bytes 1572864 | tf_op jit(solution)/shard_map/all_to_all | solution.py:49
  84.8 2.5 %copy-start.1 = (bf16[1536,128]{1,0:T(8,128)(2,1)S(1)}, bf16[1536,128]{1,0:T(8,128)(2,1)}, u32[]{:S(2)}) copy-start(bf16[1536,128]{1,0:T(8,128)(2,1)} %pad_maximum_fusion.1) | copy-start | bytes 1179652
  166.6 29.4 %copy-start.2 = (bf16[6,512,128]{2,1,0:T(8,128)(2,1)S(1)}, bf16[6,512,128]{2,1,0:T(8,128)(2,1)}, u32[]{:S(2)}) copy-start(bf16[6,512,128]{2,1,0:T(8,128)(2,1)} %get-tuple-element.69) | copy-start | bytes 2359300
  166.7 6.2 %collective-permute-start.4 = (bf16[512,128]{1,0:T(8,128)(2,1)S(1)}, bf16[512,128]{1,0:T(8,128)(2,1)S(1)}, u32[]{:S(2)}, u32[]{:S(2)}) collective-permute-start(bf16[512,128]{1,0:T(8,128)(2,1)S(1)} %get-tuple-element.177), channel_id=1, source_target_pairs={{8,0},{16,8},{24,16},{32,24},{40,32},{48,40},{56,48},{64,56},{72,6... | collective-permute-start | bytes 393224 | tf_op jit(solution)/shard_map/ppermute | solution.py:15
  168.1 11.2 %collective-permute-start.5 = (bf16[512,128]{1,0:T(8,128)(2,1)S(1)}, bf16[512,128]{1,0:T(8,128)(2,1)S(1)}, u32[]{:S(2)}, u32[]{:S(2)}) collective-permute-start(bf16[512,128]{1,0:T(8,128)(2,1)S(1)} %get-tuple-element.178), channel_id=1, source_target_pairs={{16,0},{24,8},{32,16},{40,24},{48,32},{56,40},{64,48},{72,56},{80,... | collective-permute-start | bytes 393224 | tf_op jit(solution)/shard_map/ppermute | solution.py:15
  169.5 17.1 %collective-permute-start.6 = (bf16[512,128]{1,0:T(8,128)(2,1)S(1)}, bf16[512,128]{1,0:T(8,128)(2,1)S(1)}, u32[]{:S(2)}, u32[]{:S(2)}) collective-permute-start(bf16[512,128]{1,0:T(8,128)(2,1)S(1)} %get-tuple-element.175), channel_id=1, source_target_pairs={{8,0},{16,8},{24,16},{32,24},{40,32},{48,40},{56,48},{64,56},{72,6... | collective-permute-start | bytes 393224 | tf_op jit(solution)/shard_map/ppermute | solution.py:15
  170.8 17.2 %collective-permute-start.7 = (bf16[512,128]{1,0:T(8,128)(2,1)S(1)}, bf16[512,128]{1,0:T(8,128)(2,1)S(1)}, u32[]{:S(2)}, u32[]{:S(2)}) collective-permute-start(bf16[512,128]{1,0:T(8,128)(2,1)S(1)} %get-tuple-element.176), channel_id=1, source_target_pairs={{16,0},{24,8},{32,16},{40,24},{48,32},{56,40},{64,48},{72,56},{80,... | collective-permute-start | bytes 393224 | tf_op jit(solution)/shard_map/ppermute | solution.py:15
  180.0 11.8 %all-to-all-start.6 = ((bf16[8,64,128]{2,1,0:T(8,128)(2,1)}), bf16[8,64,128]{2,1,0:T(8,128)(2,1)S(1)}, u32[]{:S(2)}, u32[]{:S(2)}) async-start(bf16[8,64,128]{2,1,0:T(8,128)(2,1)} %bitcast.18), calls=%async_computation.6 | async-start | bytes 262144 | tf_op jit(solution)/shard_map/all_to_all | solution.py:136
  191.8 9.4 %all-to-all-start.7 = ((bf16[8,64,128]{2,1,0:T(8,128)(2,1)}), bf16[8,64,128]{2,1,0:T(8,128)(2,1)S(1)}, u32[]{:S(2)}, u32[]{:S(2)}) async-start(bf16[8,64,128]{2,1,0:T(8,128)(2,1)} %bitcast.24), calls=%async_computation.7 | async-start | bytes 262144 | tf_op jit(solution)/shard_map/all_to_all | solution.py:139
  201.3 16.6 %all-to-all-start.5 = ((bf16[8,64,768]{2,1,0:T(8,128)(2,1)}), bf16[8,64,768]{2,1,0:T(8,128)(2,1)S(1)}, u32[]{:S(2)}, u32[]{:S(2)}) async-start(bf16[8,64,768]{2,1,0:T(8,128)(2,1)} %convert_element_type.70), calls=%async_computation.5 | async-start | bytes 1572864 | tf_op jit(solution)/shard_map/all_to_all | solution.py:133
where the time goes:
time: 222 us; the launch traced here: 219 us
  matrix products  66.3 us (30%)
  starting transfers between devices  62 us (28%)
  waiting for transfers between devices  50.2 us (23%)
  local copies, waits for them, and re-layouts  22 us (10%)
  other arithmetic  17.4 us (8%)
    dot_general x6, matrix products, head_partials(): jnp.dot(probs_low.T, grad_part, preferred_element_type=jnp.float32)  19.2 us
    ppermute x8, starting transfers between devices, shifted(): return lax.ppermute(block, axis, route)  18.1 us
    dot_general x6, matrix products, head_partials(): jnp.dot(grad_scores.T, query_part, preferred_element_type=jnp.float32)  14.4 us
    dot_general x6, matrix products, head_partials(): jnp.dot(grad_part, value_part.T, preferred_element_type=jnp.float32)  14 us
    all_to_all x1, waiting for transfers between devices, local(): lax.all_to_all(queries, 'head', split_axis=1, concat_axis=0, tiled=True)  11.4 us
    dot_general x6, matrix products, probabilities(): jnp.dot(query_part, key_part.T, preferred_element_type=jnp.float32)  11.2 us
    all_to_all x1, waiting for transfers between devices, local(): lax.all_to_all(grad_q.astype(jnp.bfloat16), 'head', split_axis=0, concat_...  11 us
    all_to_all x1, starting transfers between devices, local(): lax.all_to_all(keys, 'head', split_axis=1, concat_axis=0, tiled=True)  10.2 us
  transfers between devices with their start and end apart: 16, of which 10 were waited for; matrix products, arithmetic and copies ran while one was open for 9% of the time, Pallas kernels for 0%

commit v1 on v0

v1 whole, which is shorter than its diff:
```python
import functools
import math

import jax
import jax.numpy as jnp
from jax import lax
from jax.experimental import pallas as pl
from jax.experimental.pallas import tpu as pltpu
from jax.sharding import PartitionSpec as P

HEAD_DIM = 128
BLOCK = 256
WINDOW = 4
MESH = pl.DeviceIdType.MESH
FAR = 1e30


def contract_last(a, b):
    return lax.dot_general(a, b, (((1,), (1,)), ((), ())), preferred_element_type=jnp.float32)


def kernel(
    parts,
    devices,
    group,
    q_hbm,
    k_hbm,
    v_hbm,
    o_hbm,
    g_hbm,
    first_ref,
    dq_hbm,
    dk_ref,
    dv_ref,
    q_own,
    g_own,
    o_own,
    corr_out,
    corr_in,
    corr_cols,
    qg,
    kv,
    k_turned,
    total,
    dq_out,
    terms,
    far_terms,
    arrived,
    load_sem,
    kv_sem,
    near_sem,
    far_sem,
    corr_sem,
    qg_sem,
    dq_sem,
    term_sem,
    far_term_sem,
    send_sem,
):
    rows = 2 * BLOCK // devices
    half = devices // 2
    width = group * HEAD_DIM
    span = 2 * BLOCK
    own = 3 * BLOCK
    scaling = HEAD_DIM ** (-0.5)
    to_exp2 = scaling * math.log2(math.e)
    p = lax.axis_index("ctx")
    h = lax.axis_index("head")

    def at(shift):
        return lax.rem(p + shift + parts, parts)

    def other(off):
        return lax.rem(h + off, devices)

    load_q = pltpu.make_async_copy(q_hbm, q_own, load_sem.at[0])
    load_g = pltpu.make_async_copy(g_hbm, g_own, load_sem.at[1])
    load_o = pltpu.make_async_copy(o_hbm, o_own, load_sem.at[2])
    load_q.start()
    load_g.start()
    load_o.start()

    barrier = pltpu.get_barrier_semaphore()

    def greet_row(off, carry):
        pl.semaphore_signal(barrier, inc=1, device_id=(p, other(off)), device_id_type=MESH)
        return carry

    def greet_near(off, carry):
        for shift in (1, -1):
            pl.semaphore_signal(
                barrier, inc=1, device_id=(at(shift), other(off)), device_id_type=MESH
            )
        return carry

    lax.fori_loop(1, devices, greet_row, 0)
    lax.fori_loop(0, devices, greet_near, 0)
    for shift in (2, -2):
        pl.semaphore_signal(barrier, inc=1, device_id=(at(shift), h), device_id_type=MESH)
    pl.semaphore_wait(barrier, 3 * devices + 1)

    def rows_at(start, count):
        return pl.ds(pl.multiple_of(start, 64), count)

    def lanes_at(start, count):
        return pl.ds(pl.multiple_of(start, HEAD_DIM), count)

    mine = rows_at(h * rows, rows)
    mine_kv = rows_at(own + h * rows, rows)

    for index, source in ((0, k_hbm), (1, v_hbm)):

        def send_kv(off, carry):
            d = other(off)
            pltpu.make_async_remote_copy(
                src_ref=source.at[:, lanes_at(d * HEAD_DIM, HEAD_DIM)],
                dst_ref=kv.at[index, mine_kv],
                send_sem=send_sem.at[0],
                recv_sem=kv_sem.at[index],
                device_id=(p, d),
                device_id_type=MESH,
            ).start()
            return carry

        lax.fori_loop(1, devices, send_kv, 0)
        pltpu.make_async_copy(
            source.at[:, lanes_at(h * HEAD_DIM, HEAD_DIM)], kv.at[index, mine_kv], kv_sem.at[index]
        ).start()

    def send_heads(i, count, sem):
        for index, source in ((0, q_own), (1, g_own)):

            def send_part(off, carry):
                d = other(off)
                pltpu.make_async_remote_copy(
                    src_ref=source.at[:, lanes_at(d * width + i * HEAD_DIM, count * HEAD_DIM)],
                    dst_ref=qg.at[index, mine, lanes_at(i * HEAD_DIM, count * HEAD_DIM)],
                    send_sem=send_sem.at[2],
                    recv_sem=qg_sem.at[sem],
                    device_id=(p, d),
                    device_id_type=MESH,
                ).start()
                return carry

            lax.fori_loop(1, devices, send_part, 0)
            pltpu.make_async_copy(
                source.at[:, lanes_at(h * width + i * HEAD_DIM, count * HEAD_DIM)],
                qg.at[index, mine, lanes_at(i * HEAD_DIM, count * HEAD_DIM)],
                qg_sem.at[sem],
            ).start()

    def wait_heads(i, count, sem):
        part = qg.at[:, :, i * HEAD_DIM : (i + count) * HEAD_DIM]
        pltpu.make_async_copy(part, part, qg_sem.at[sem]).wait()

    load_q.wait()
    load_g.wait()
    send_heads(0, 2, 0)


    load_o.wait()
    row_of = lax.broadcasted_iota(jnp.int32, (16, width), 0)
    col_of = lax.broadcasted_iota(jnp.int32, (16, width), 1)
    pick = jnp.where((row_of % 8) == col_of // HEAD_DIM, 1.0, 0.0).astype(jnp.bfloat16)
    upper = lax.broadcasted_iota(jnp.int32, (16, rows), 0) < 8
    corr_out[...] = jnp.zeros_like(corr_out)
    for d in range(devices):
        cols = slice(d * width, (d + 1) * width)
        product = g_own[:, cols].astype(jnp.float32) * o_own[:, cols].astype(jnp.float32)
        high = product.astype(jnp.bfloat16)
        low = (product - high.astype(jnp.float32)).astype(jnp.bfloat16)
        corr = contract_last(pick, high) + contract_last(pick, low)
        corr_high = corr.astype(jnp.bfloat16).astype(jnp.float32)
        corr_out[d, :, 0:rows] = jnp.where(upper, corr_high, corr - corr_high).astype(jnp.bfloat16)

    def send_corr(off, carry):
        d = other(off)
        pltpu.make_async_remote_copy(
            src_ref=corr_out.at[d],
            dst_ref=corr_in.at[h],
            send_sem=send_sem.at[1],
            recv_sem=corr_sem,
            device_id=(p, d),
            device_id_type=MESH,
        ).start()
        return carry

    lax.fori_loop(1, devices, send_corr, 0)
    pltpu.make_async_copy(corr_out.at[h], corr_in.at[h], corr_sem).start()
    total[...] = jnp.zeros_like(total)

    total[...] = jnp.zeros_like(total)

    near, far = [], []
    for index in range(2):
        held = kv.at[index, own : own + span]
        pltpu.make_async_copy(held, held, kv_sem.at[index]).wait()
        near.append(
            pltpu.make_async_remote_copy(
                src_ref=held,
                dst_ref=kv.at[index, BLOCK : BLOCK + span],
                send_sem=send_sem.at[3],
                recv_sem=near_sem.at[index],
                device_id=(at(1), h),
                device_id_type=MESH,
            )
        )
        near[index].start()
        far.append(
            pltpu.make_async_remote_copy(
                src_ref=kv.at[index, 2 * BLOCK : 3 * BLOCK],
                dst_ref=kv.at[index, 0:BLOCK],
                send_sem=send_sem.at[4],
                recv_sem=far_sem.at[index],
                device_id=(at(1), h),
                device_id_type=MESH,
            )
        )
    total[...] = jnp.zeros_like(total)
    send_heads(2, 2, 1)

    for index in range(2):
        near[index].wait_recv()
        far[index].start()
    send_heads(4, 1, 2)
    send_heads(5, 1, 3)

    pltpu.make_async_copy(corr_in, corr_in, corr_sem).wait()
    for d in range(devices):
        piece = corr_in[d].astype(jnp.float32)
        square = jnp.concatenate([piece, jnp.zeros((112, HEAD_DIM), jnp.float32)], axis=0).T
        corr_cols[d * rows : (d + 1) * rows] = square[0:rows].astype(jnp.bfloat16)

    def turn(block):
        part = slice(block * BLOCK, (block + 1) * BLOCK)
        k_turned[:, part] = kv[0, part].astype(jnp.float32).T.astype(jnp.bfloat16)

    turn(3)
    turn(4)
    turn(1)
    turn(2)

    def round_terms(start, count):
        for r in range(start, start + count):
            part = slice(r * rows, (r + 1) * rows)
            terms[r, 0] = (total[0, part] * scaling).astype(jnp.bfloat16)
            terms[r, 1] = total[1, part].astype(jnp.bfloat16)

    def term_copy(r, distance, d):
        return pltpu.make_async_remote_copy(
            src_ref=terms.at[r],
            dst_ref=arrived.at[distance, h],
            send_sem=send_sem.at[6],
            recv_sem=term_sem.at[distance],
            device_id=(at(-distance), d),
            device_id_type=MESH,
        )

    pass_back = pltpu.make_async_remote_copy(
        src_ref=terms.at[0:half],
        dst_ref=far_terms,
        send_sem=send_sem.at[7],
        recv_sem=far_term_sem,
        device_id=(at(-2), h),
        device_id_type=MESH,
    )

    def send_dq(i, count):
        cols = slice(i * HEAD_DIM, (i + count) * HEAD_DIM)
        target = dq_hbm.at[:, lanes_at(h * width + i * HEAD_DIM, count * HEAD_DIM)]

        def send_part(off, carry):
            d = other(off)
            pltpu.make_async_remote_copy(
                src_ref=dq_out.at[rows_at(d * rows, rows), cols],
                dst_ref=target,
                send_sem=send_sem.at[5],
                recv_sem=dq_sem,
                device_id=(p, d),
                device_id_type=MESH,
            ).start()
            return carry

        lax.fori_loop(1, devices, send_part, 0)
        pltpu.make_async_copy(dq_out.at[mine, cols], target, dq_sem).start()

    def send_half(i, count, late):
        cols = slice(i * HEAD_DIM, (i + count) * HEAD_DIM)
        target = dq_hbm.at[:, lanes_at(h * width + i * HEAD_DIM, count * HEAD_DIM)]

        def send_part(d, carry):
            source = dq_out.at[rows_at(d * rows, rows), cols]

            @pl.when(d != h)
            def _():
                pltpu.make_async_remote_copy(
                    src_ref=source,
                    dst_ref=target,
                    send_sem=send_sem.at[5],
                    recv_sem=dq_sem,
                    device_id=(p, d),
                    device_id_type=MESH,
                ).start()

            @pl.when(d == h)
            def _():
                pltpu.make_async_copy(source, target, dq_sem).start()

            return carry

        lax.fori_loop(late * half, (late + 1) * half, send_part, 0)

    reach = WINDOW * BLOCK
    lane = lax.broadcasted_iota(jnp.int32, (reach, HEAD_DIM), 1)

    def products(late, i):
        query_rows = rows_at(late * BLOCK, BLOCK)
        key_rows = rows_at(late * BLOCK, reach)
        head_cols = lanes_at(i * HEAD_DIM, HEAD_DIM)
        q = qg[0, query_rows, head_cols]
        g = qg[1, query_rows, head_cols]
        score = contract_last(kv[0, key_rows, :], q)
        g_wide = jnp.concatenate([g, corr_cols[query_rows, :]], axis=1)
        minus = jnp.where((lane == i) | (lane == i + 8), -1.0, 0.0).astype(jnp.bfloat16)
        v_wide = jnp.concatenate([kv[1, key_rows, :], minus], axis=1)
        return q, g, score, contract_last(v_wide, g_wide)

    def softmax(late, score):
        first = first_ref[2 * p + late]
        tiles = [score[t * BLOCK : (t + 1) * BLOCK] for t in range(WINDOW)]
        biases = [
            jnp.where(first <= 2 * p + late - 3 + t, 0.0, -FAR).astype(jnp.float32)
            for t in range(WINDOW)
        ]
        peak = None
        for t in range(WINDOW):
            top = jnp.max(tiles[t], axis=0, keepdims=True) + biases[t]
            peak = top if peak is None else jnp.maximum(peak, top)
        level = peak * to_exp2
        weights = [
            jnp.exp2(tiles[t] * to_exp2 - (level - biases[t])) for t in range(WINDOW)
        ]
        weights = jnp.concatenate(weights, axis=0)
        return weights * (1.0 / jnp.sum(weights, axis=0, keepdims=True))

    def returned(late, i, q, g, probs, grads):
        grad_scores = (probs * grads).astype(jnp.bfloat16)
        key_term = jnp.dot(grad_scores, q, preferred_element_type=jnp.float32)
        value_term = jnp.dot(probs.astype(jnp.bfloat16), g, preferred_element_type=jnp.float32)
        dq_turned = jnp.dot(
            k_turned[:, lanes_at(late * BLOCK, reach)],
            grad_scores,
            preferred_element_type=jnp.float32,
        )
        query_rows = rows_at(late * BLOCK, BLOCK)
        dq_out[query_rows, lanes_at(i * HEAD_DIM, HEAD_DIM)] = (
            (dq_turned * scaling).T.astype(jnp.bfloat16)
        )
        key_rows = rows_at(late * BLOCK, reach)
        total[0, key_rows, :] += key_term
        total[1, key_rows, :] += value_term

    def pair(k, carry):
        late = (5 - k) // 5 + k // 5
        late_b = k % 2 + (5 - k) // 5
        i = k - ((k + 1) // 2) % 2
        i_b = k + (k // 2 + 1) % 2 - k // 5

        @pl.when(k == 1)
        def _():
            far[0].wait_recv()
            far[1].wait_recv()
            turn(0)
            wait_heads(2, 2, 1)

        @pl.when(k == 4)
        def _():
            wait_heads(4, 1, 2)
            wait_heads(5, 1, 3)

        q, g, score, grads = products(late, i)
        q_b, g_b, score_b, grads_b = products(late_b, i_b)
        probs = softmax(late, score)
        probs_b = softmax(late_b, score_b)
        returned(late, i, q, g, probs, grads)
        returned(late_b, i_b, q_b, g_b, probs_b, grads_b)

        @pl.when(k == 2)
        def _():
            send_dq(0, 2)

        @pl.when(k == 3)
        def _():
            send_dq(2, 2)

        @pl.when(k == 4)
        def _():
            round_terms(0, half)
            pass_back.start()
            send_half(4, 2, 0)

        return carry

    wait_heads(0, 2, 0)
    lax.fori_loop(0, group, pair, 0)

    round_terms(half, devices)

    def send_near(off, carry):
        d = other(off)
        term_copy(half + d, 1, d).start()
        return carry

    lax.fori_loop(0, devices, send_near, 0)
    send_half(4, 2, 1)
    def send_own(d, carry):
        source = terms.at[half + devices + d]

        @pl.when(d != h)
        def _():
            term_copy(half + devices + d, 0, d).start()

        @pl.when(d == h)
        def _():
            pltpu.make_async_copy(source, arrived.at[0, h], term_sem.at[0]).start()

        return carry

    round_terms(half + devices, half)
    lax.fori_loop(0, half, send_own, 0)
    pass_back.wait_recv()
    for r in range(half):
        at_row = half + devices + half + r
        part = slice(at_row * rows, (at_row + 1) * rows)
        terms[at_row, 0] = (
            total[0, part] * scaling + far_terms[r, 0].astype(jnp.float32)
        ).astype(jnp.bfloat16)
        terms[at_row, 1] = (total[1, part] + far_terms[r, 1].astype(jnp.float32)).astype(
            jnp.bfloat16
        )
    lax.fori_loop(half, devices, send_own, 0)

    pltpu.make_async_copy(arrived.at[0], arrived.at[0], term_sem.at[0]).wait()
    pltpu.make_async_copy(arrived.at[1], arrived.at[1], term_sem.at[1]).wait()
    for d in range(devices):
        cols = slice(d * HEAD_DIM, (d + 1) * HEAD_DIM)
        for index, out in ((0, dk_ref), (1, dv_ref)):
            held = arrived[0, d, index].astype(jnp.float32)
            more = arrived[1, d, index].astype(jnp.float32)
            out[:, cols] = (held + more).astype(jnp.bfloat16)
    pltpu.make_async_copy(dq_hbm, dq_hbm, dq_sem).wait()

    most = span - rows

    def left(view, index):
        pltpu.make_async_copy(view, view, send_sem.at[index]).wait()

    left(kv.at[:, 0:most], 0)
    left(corr_in.at[0 : devices - 1], 1)
    left(qg.at[:, 0:most], 2)
    left(kv.at[:, 0:span], 3)
    left(kv.at[:, 0:BLOCK], 4)
    pass_back.wait_send()
    left(dq_out.at[0:most], 5)
    left(terms.at[0 : 2 * devices - 1], 6)


def solution(mesh):
    parts = mesh.shape["ctx"]
    devices = mesh.shape["head"]
    rows = 2 * BLOCK // devices

    def local(queries, keys, values, outputs, grad_out, first_block):
        group = queries.shape[1] // keys.shape[1]
        hbm = pl.BlockSpec(memory_space=pl.ANY)
        vmem = pl.BlockSpec(memory_space=pltpu.VMEM)
        low, full = jnp.bfloat16, jnp.float32
        dma = pltpu.SemaphoreType.DMA
        width = queries.shape[1] // devices
        band = 5 * BLOCK
        return pl.pallas_call(
            functools.partial(kernel, parts, devices, group),
            out_shape=(
                jax.ShapeDtypeStruct(queries.shape, low),
                jax.ShapeDtypeStruct(keys.shape, low),
                jax.ShapeDtypeStruct(values.shape, low),
            ),
            in_specs=[hbm] * 5 + [pl.BlockSpec(memory_space=pltpu.SMEM)],
            out_specs=(hbm, vmem, vmem),
            scratch_shapes=[
                pltpu.VMEM(queries.shape, low),
                pltpu.VMEM(grad_out.shape, low),
                pltpu.VMEM(outputs.shape, low),
                pltpu.VMEM((devices, 16, HEAD_DIM), low),
                pltpu.VMEM((devices, 16, HEAD_DIM), low),
                pltpu.VMEM((2 * BLOCK, HEAD_DIM), low),
                pltpu.VMEM((2, 2 * BLOCK, width), low),
                pltpu.VMEM((2, band, HEAD_DIM), low),
                pltpu.VMEM((HEAD_DIM, band), low),
                pltpu.VMEM((2, band, HEAD_DIM), full),
                pltpu.VMEM((2 * BLOCK, width), low),
                pltpu.VMEM((band // rows, 2, rows, HEAD_DIM), low),
                pltpu.VMEM((devices // 2, 2, rows, HEAD_DIM), low),
                pltpu.VMEM((2, devices, 2, rows, HEAD_DIM), low),
                dma((3,)),
                dma((2,)),
                dma((2,)),
                dma((2,)),
                dma,
                dma((4,)),
                dma,
                dma((2,)),
                dma,
                dma((8,)),
            ],
            compiler_params=pltpu.CompilerParams(
                collective_id=0,
                has_side_effects=True,
                vmem_limit_bytes=63 * 1024 * 1024,
            ),
            cost_estimate=pl.CostEstimate(
                flops=48 * 5 * 2 * 256 * 256 * 128, bytes_accessed=8_000_000, transcendentals=0
            ),
        )(queries, keys, values, outputs, grad_out, first_block)

    placed = P(("ctx", "head"), None)
    return jax.shard_map(
        local,
        mesh=mesh,
        in_specs=(placed,) * 5 + (P(),),
        out_specs=(placed,) * 3,
        check_vma=False,
    )
```

time: 222 us -> 61.2 us (0.28); the launches traced: 219 us -> 61 us
  matrix products: 66.3 us -> 0 us
  starting transfers between devices: 62 us -> 0 us
  Pallas kernels: 0 us -> 56.7 us
  waiting for transfers between devices: 50.2 us -> 0 us
  local copies, waits for them, and re-layouts: 22 us -> 3.71 us
  other arithmetic: 17.4 us -> 0 us
    dot_general x30 -> x0, matrix products: 66.3 us -> none  [the longest x6 19.2 us: head_partials(): jnp.dot(probs_low.T, grad_part, preferred_element_type=jnp.float32)]
    pallas_call x0 -> x1, Pallas kernels: none -> 56.7 us  [local(): pl.pallas_call(functools.partial(kernel, parts, devices, group), out_shap...]
    all_to_all x8 -> x0, starting transfers between devices: 43.9 us -> none  [the longest x1 10.2 us: local(): lax.all_to_all(keys, 'head', split_axis=1, concat_axis=0, tiled=True)]
    all_to_all x8 -> x0, waiting for transfers between devices: 41.6 us -> none  [the longest x1 11.4 us: local(): lax.all_to_all(queries, 'head', split_axis=1, concat_axis=0, tiled=True)]
    ppermute x8 -> x0, starting transfers between devices: 18.1 us -> none  [shifted(): return lax.ppermute(block, axis, route)]
    reduce_sum x9 -> x0, other arithmetic: 11.8 us -> none  [the longest x6 5.87 us: probabilities(): row_total = jnp.sum(weights, axis=1, keepdims=True)]
    ppermute x8 -> x0, waiting for transfers between devices: 8.61 us -> none  [shifted(): return lax.ppermute(block, axis, route)]
    all_to_all x8 -> x0, local copies, waits for them, and re-layouts: 8.55 us -> none  [the longest x1 2.14 us: local(): lax.all_to_all(queries, 'head', split_axis=1, concat_axis=0, tiled=True)]
  transfers between devices with their start and end apart: 16 -> 0, of which waited for: 10 -> 0; matrix products, arithmetic and copies ran while one was open for 9% -> 0% of each run, Pallas kernels for 0% -> 0%
where the time goes in v1:
time: 61.2 us; the launch traced here: 61 us
  Pallas kernels  56.7 us (93%)
  local copies, waits for them, and re-layouts  3.71 us (6%)
  between operations  0.65 us (1%)
    pallas_call x1, Pallas kernels, local(): pl.pallas_call(functools.partial(kernel, parts, devices, group), out_shap...  56.7 us
    unnamed x7, local copies, waits for them, and re-layouts  3.71 us

profile of v1, /device:TPU:1, one launch (start us, length us, event | category | flops | bytes accessed | tf_op | source)
XLA Modules:
  0.0 61.0 jit_solution(6318806460754154780)
XLA Ops:
  0.6 56.7 %shard_map.85 = (bf16[64,6144]{1,0:T(8,128)(2,1)}, bf16[64,1024]{1,0:T(8,128)(2,1)}, bf16[64,1024]{1,0:T(8,128)(2,1)}) custom-call(bf16[64,6144]{1,0:T(8,128)(2,1)} %q_hbm.1, bf16[64,1024]{1,0:T(8,128)(2,1)} %k_hbm.1, bf16[64,1024]{1,0:T(8,128)(2,1)} %v_hbm.1, bf16[64,6144]{1,0:T(8,128)(2,1)} %o_hbm.1, bf16[64,6144]{1,0:T(8,128)(2,1)} %g_hbm.1, s32[128]{0:T(128)} %first_ref.1), custom_call_target="tpu_custom_call" | custom-call | flops 4026531840 | bytes 8000000 | tf_op jit(solution)/shard_map/pallas_call | solution.py:481
  57.3 0.0 copy-start.1
  57.3 2.1 %copy.12 = bf16[64,6144]{1,0:T(8,128)(2,1)} copy(bf16[64,6144]{1,0:T(8,128)(2,1)} %get-tuple-element.6) | data formatting | bytes 1572864
  59.4 0.0 copy-done.1
  59.4 0.0 copy-start
  59.4 0.7 %copy.13 = bf16[64,1024]{1,0:T(8,128)(2,1)} copy(bf16[64,1024]{1,0:T(8,128)(2,1)S(1)} %copy-done.1) | data formatting | bytes 262144
  60.1 0.3 copy-done
  60.4 0.7 %copy.14 = bf16[64,1024]{1,0:T(8,128)(2,1)} copy(bf16[64,1024]{1,0:T(8,128)(2,1)S(1)} %copy-done) | data formatting | bytes 262144
Async XLA Ops:
  57.3 2.1 %copy-start.1 = (bf16[64,1024]{1,0:T(8,128)(2,1)S(1)}, bf16[64,1024]{1,0:T(8,128)(2,1)}, u32[]{:S(2)}) copy-start(bf16[64,1024]{1,0:T(8,128)(2,1)} %get-tuple-element.7) | copy-start | bytes 393220
  59.4 1.0 %copy-start = (bf16[64,1024]{1,0:T(8,128)(2,1)S(1)}, bf16[64,1024]{1,0:T(8,128)(2,1)}, u32[]{:S(2)}) copy-start(bf16[64,1024]{1,0:T(8,128)(2,1)} %get-tuple-element.8) | copy-start | bytes 393220

commit v2 on v1

--- a/solution.py
+++ b/solution.py
@@ -30,8 +30,7 @@
     g_hbm,
     first_ref,
     dq_hbm,
-    dk_ref,
-    dv_ref,
+    dkv_ref,
     q_own,
     g_own,
     o_own,
@@ -39,7 +38,8 @@
     corr_in,
     corr_cols,
     qg,
-    kv,
+    k_band,
+    v_band,
     k_turned,
     total,
     dq_out,
@@ -108,13 +108,13 @@
     mine = rows_at(h * rows, rows)
     mine_kv = rows_at(own + h * rows, rows)
 
-    for index, source in ((0, k_hbm), (1, v_hbm)):
+    for index, source, band in ((0, k_hbm, k_band), (1, v_hbm, v_band)):
 
         def send_kv(off, carry):
             d = other(off)
             pltpu.make_async_remote_copy(
                 src_ref=source.at[:, lanes_at(d * HEAD_DIM, HEAD_DIM)],
-                dst_ref=kv.at[index, mine_kv],
+                dst_ref=band.at[mine_kv, 0:HEAD_DIM],
                 send_sem=send_sem.at[0],
                 recv_sem=kv_sem.at[index],
                 device_id=(p, d),
@@ -124,7 +124,7 @@
 
         lax.fori_loop(1, devices, send_kv, 0)
         pltpu.make_async_copy(
-            source.at[:, lanes_at(h * HEAD_DIM, HEAD_DIM)], kv.at[index, mine_kv], kv_sem.at[index]
+            source.at[:, lanes_at(h * HEAD_DIM, HEAD_DIM)], band.at[mine_kv, 0:HEAD_DIM], kv_sem.at[index]
         ).start()
 
     def send_heads(i, count, sem):
@@ -188,17 +188,17 @@
     lax.fori_loop(1, devices, send_corr, 0)
     pltpu.make_async_copy(corr_out.at[h], corr_in.at[h], corr_sem).start()
     total[...] = jnp.zeros_like(total)
-
-    total[...] = jnp.zeros_like(total)
+    v_band[:, HEAD_DIM:] = jnp.full((5 * BLOCK, HEAD_DIM), -1.0, jnp.bfloat16)
+
 
     near, far = [], []
-    for index in range(2):
-        held = kv.at[index, own : own + span]
+    for index, band in ((0, k_band), (1, v_band)):
+        held = band.at[own : own + span, 0:HEAD_DIM]
         pltpu.make_async_copy(held, held, kv_sem.at[index]).wait()
         near.append(
             pltpu.make_async_remote_copy(
                 src_ref=held,
-                dst_ref=kv.at[index, BLOCK : BLOCK + span],
+                dst_ref=band.at[BLOCK : BLOCK + span, 0:HEAD_DIM],
                 send_sem=send_sem.at[3],
                 recv_sem=near_sem.at[index],
                 device_id=(at(1), h),
@@ -208,22 +208,26 @@
         near[index].start()
         far.append(
             pltpu.make_async_remote_copy(
-                src_ref=kv.at[index, 2 * BLOCK : 3 * BLOCK],
-                dst_ref=kv.at[index, 0:BLOCK],
+                src_ref=band.at[2 * BLOCK : 3 * BLOCK, 0:HEAD_DIM],
+                dst_ref=band.at[0:BLOCK, 0:HEAD_DIM],
                 send_sem=send_sem.at[4],
                 recv_sem=far_sem.at[index],
                 device_id=(at(1), h),
                 device_id_type=MESH,
             )
         )
-    total[...] = jnp.zeros_like(total)
     send_heads(2, 2, 1)
 
-    for index in range(2):
-        near[index].wait_recv()
-        far[index].start()
-    send_heads(4, 1, 2)
-    send_heads(5, 1, 3)
+    def turn(block):
+        part = slice(block * BLOCK, (block + 1) * BLOCK)
+        k_turned[:, part] = k_band[part].astype(jnp.float32).T.astype(jnp.bfloat16)
+
+    turn(3)
+    turn(4)
+    near[0].wait_recv()
+    far[0].start()
+    turn(1)
+    turn(2)
 
     pltpu.make_async_copy(corr_in, corr_in, corr_sem).wait()
     for d in range(devices):
@@ -231,14 +235,10 @@
         square = jnp.concatenate([piece, jnp.zeros((112, HEAD_DIM), jnp.float32)], axis=0).T
         corr_cols[d * rows : (d + 1) * rows] = square[0:rows].astype(jnp.bfloat16)
 
-    def turn(block):
-        part = slice(block * BLOCK, (block + 1) * BLOCK)
-        k_turned[:, part] = kv[0, part].astype(jnp.float32).T.astype(jnp.bfloat16)
-
-    turn(3)
-    turn(4)
-    turn(1)
-    turn(2)
+    near[1].wait_recv()
+    far[1].start()
+    send_heads(4, 2, 2)
+
 
     def round_terms(start, count):
         for r in range(start, start + count):
@@ -311,21 +311,41 @@
         lax.fori_loop(late * half, (late + 1) * half, send_part, 0)
 
     reach = WINDOW * BLOCK
-    lane = lax.broadcasted_iota(jnp.int32, (reach, HEAD_DIM), 1)
-
-    def products(late, i):
+    lane = lax.broadcasted_iota(jnp.int32, (BLOCK, HEAD_DIM), 1)
+
+    def pair(k, carry):
+        late = ((k + 1) % 2) * (1 - k // 4) + (k // 4) * (k % 2)
+        i = 2 * (k // 2)
+
+        @pl.when(k == 1)
+        def _():
+            far[0].wait_recv()
+            far[1].wait_recv()
+            turn(0)
+
+        @pl.when(k == 2)
+        def _():
+            wait_heads(2, 2, 1)
+
+        @pl.when(k == 4)
+        def _():
+            wait_heads(4, 2, 2)
+
         query_rows = rows_at(late * BLOCK, BLOCK)
         key_rows = rows_at(late * BLOCK, reach)
-        head_cols = lanes_at(i * HEAD_DIM, HEAD_DIM)
-        q = qg[0, query_rows, head_cols]
-        g = qg[1, query_rows, head_cols]
-        score = contract_last(kv[0, key_rows, :], q)
-        g_wide = jnp.concatenate([g, corr_cols[query_rows, :]], axis=1)
-        minus = jnp.where((lane == i) | (lane == i + 8), -1.0, 0.0).astype(jnp.bfloat16)
-        v_wide = jnp.concatenate([kv[1, key_rows, :], minus], axis=1)
-        return q, g, score, contract_last(v_wide, g_wide)
-
-    def softmax(late, score):
+        heads = [lanes_at((i + n) * HEAD_DIM, HEAD_DIM) for n in range(2)]
+        q = jnp.concatenate([qg[0, query_rows, cols] for cols in heads], axis=0)
+        g = jnp.concatenate([qg[1, query_rows, cols] for cols in heads], axis=0)
+        corr = corr_cols[query_rows, :].astype(jnp.float32)
+        corr = jnp.concatenate(
+            [
+                jnp.where((lane == i + n) | (lane == i + n + 8), corr, 0.0).astype(jnp.bfloat16)
+                for n in range(2)
+            ],
+            axis=0,
+        )
+        score = contract_last(k_band[key_rows, :], q)
+        grads = contract_last(v_band[key_rows, :], jnp.concatenate([g, corr], axis=1))
         first = first_ref[2 * p + late]
         tiles = [score[t * BLOCK : (t + 1) * BLOCK] for t in range(WINDOW)]
         biases = [
@@ -341,51 +361,22 @@
             jnp.exp2(tiles[t] * to_exp2 - (level - biases[t])) for t in range(WINDOW)
         ]
         weights = jnp.concatenate(weights, axis=0)
-        return weights * (1.0 / jnp.sum(weights, axis=0, keepdims=True))
-
-    def returned(late, i, q, g, probs, grads):
+        probs = weights * (1.0 / jnp.sum(weights, axis=0, keepdims=True))
         grad_scores = (probs * grads).astype(jnp.bfloat16)
-        key_term = jnp.dot(grad_scores, q, preferred_element_type=jnp.float32)
-        value_term = jnp.dot(probs.astype(jnp.bfloat16), g, preferred_element_type=jnp.float32)
+        total[0, key_rows, :] += jnp.dot(grad_scores, q, preferred_element_type=jnp.float32)
+        total[1, key_rows, :] += jnp.dot(
+            probs.astype(jnp.bfloat16), g, preferred_element_type=jnp.float32
+        )
         dq_turned = jnp.dot(
             k_turned[:, lanes_at(late * BLOCK, reach)],
             grad_scores,
             preferred_element_type=jnp.float32,
         )
-        query_rows = rows_at(late * BLOCK, BLOCK)
-        dq_out[query_rows, lanes_at(i * HEAD_DIM, HEAD_DIM)] = (
-            (dq_turned * scaling).T.astype(jnp.bfloat16)
-        )
-        key_rows = rows_at(late * BLOCK, reach)
-        total[0, key_rows, :] += key_term
-        total[1, key_rows, :] += value_term
-
-    def pair(k, carry):
-        late = (5 - k) // 5 + k // 5
-        late_b = k % 2 + (5 - k) // 5
-        i = k - ((k + 1) // 2) % 2
-        i_b = k + (k // 2 + 1) % 2 - k // 5
+        dq = (dq_turned * scaling).T.astype(jnp.bfloat16)
+        for n in range(2):
+            dq_out[query_rows, heads[n]] = dq[n * BLOCK : (n + 1) * BLOCK]
 
         @pl.when(k == 1)
-        def _():
-            far[0].wait_recv()
-            far[1].wait_recv()
-            turn(0)
-            wait_heads(2, 2, 1)
-
-        @pl.when(k == 4)
-        def _():
-            wait_heads(4, 1, 2)
-            wait_heads(5, 1, 3)
-
-        q, g, score, grads = products(late, i)
-        q_b, g_b, score_b, grads_b = products(late_b, i_b)
-        probs = softmax(late, score)
-        probs_b = softmax(late_b, score_b)
-        returned(late, i, q, g, probs, grads)
-        returned(late_b, i_b, q_b, g_b, probs_b, grads_b)
-
-        @pl.when(k == 2)
         def _():
             send_dq(0, 2)
 
@@ -444,10 +435,10 @@
     pltpu.make_async_copy(arrived.at[1], arrived.at[1], term_sem.at[1]).wait()
     for d in range(devices):
         cols = slice(d * HEAD_DIM, (d + 1) * HEAD_DIM)
-        for index, out in ((0, dk_ref), (1, dv_ref)):
+        for index in range(2):
             held = arrived[0, d, index].astype(jnp.float32)
             more = arrived[1, d, index].astype(jnp.float32)
-            out[:, cols] = (held + more).astype(jnp.bfloat16)
+            dkv_ref[index, :, cols] = (held + more).astype(jnp.bfloat16)
     pltpu.make_async_copy(dq_hbm, dq_hbm, dq_sem).wait()
 
     most = span - rows
@@ -455,14 +446,34 @@
     def left(view, index):
         pltpu.make_async_copy(view, view, send_sem.at[index]).wait()
 
-    left(kv.at[:, 0:most], 0)
+    left(k_band.at[0 : 2 * most], 0)
     left(corr_in.at[0 : devices - 1], 1)
     left(qg.at[:, 0:most], 2)
-    left(kv.at[:, 0:span], 3)
-    left(kv.at[:, 0:BLOCK], 4)
+    left(k_band.at[0 : 2 * span], 3)
+    left(k_band.at[0 : 2 * BLOCK], 4)
     pass_back.wait_send()
     left(dq_out.at[0:most], 5)
     left(terms.at[0 : 2 * devices - 1], 6)
+
+
+def finish(pieces, dq, dkv, dq_hbm, dk_hbm, dv_hbm, held, held_kv, in_sem, out_sem):
+    rows = held.shape[0] // pieces
+    legs = []
+    for n in range(pieces):
+        part = slice(n * rows, (n + 1) * rows)
+        legs.append((dq.at[part], held.at[part], dq_hbm.at[part]))
+    legs.append((dkv.at[0], held_kv.at[0], dk_hbm))
+    legs.append((dkv.at[1], held_kv.at[1], dv_hbm))
+    loads, stores = [], []
+    for n, (source, between, target) in enumerate(legs):
+        loads.append(pltpu.make_async_copy(source, between, in_sem.at[n]))
+        stores.append(pltpu.make_async_copy(between, target, out_sem.at[n]))
+        loads[n].start()
+    for n in range(len(legs)):
+        loads[n].wait()
+        stores[n].start()
+    for n in range(len(legs)):
+        stores[n].wait()
 
 
 def solution(mesh):
@@ -477,16 +488,16 @@
         low, full = jnp.bfloat16, jnp.float32
         dma = pltpu.SemaphoreType.DMA
         width = queries.shape[1] // devices
+        pieces = 4
         band = 5 * BLOCK
-        return pl.pallas_call(
+        dq, dkv = pl.pallas_call(
             functools.partial(kernel, parts, devices, group),
             out_shape=(
                 jax.ShapeDtypeStruct(queries.shape, low),
-                jax.ShapeDtypeStruct(keys.shape, low),
-                jax.ShapeDtypeStruct(values.shape, low),
+                jax.ShapeDtypeStruct((2, *keys.shape), low),
             ),
             in_specs=[hbm] * 5 + [pl.BlockSpec(memory_space=pltpu.SMEM)],
-            out_specs=(hbm, vmem, vmem),
+            out_specs=(hbm, vmem),
             scratch_shapes=[
                 pltpu.VMEM(queries.shape, low),
                 pltpu.VMEM(grad_out.shape, low),
@@ -495,7 +506,8 @@
                 pltpu.VMEM((devices, 16, HEAD_DIM), low),
                 pltpu.VMEM((2 * BLOCK, HEAD_DIM), low),
                 pltpu.VMEM((2, 2 * BLOCK, width), low),
-                pltpu.VMEM((2, band, HEAD_DIM), low),
+                pltpu.VMEM((band, HEAD_DIM), low),
+                pltpu.VMEM((band, 2 * HEAD_DIM), low),
                 pltpu.VMEM((HEAD_DIM, band), low),
                 pltpu.VMEM((2, band, HEAD_DIM), full),
                 pltpu.VMEM((2 * BLOCK, width), low),
@@ -507,7 +519,7 @@
                 dma((2,)),
                 dma((2,)),
                 dma,
-                dma((4,)),
+                dma((3,)),
                 dma,
                 dma((2,)),
                 dma,
@@ -522,6 +534,23 @@
                 flops=48 * 5 * 2 * 256 * 256 * 128, bytes_accessed=8_000_000, transcendentals=0
             ),
         )(queries, keys, values, outputs, grad_out, first_block)
+        return pl.pallas_call(
+            functools.partial(finish, pieces),
+            out_shape=(
+                jax.ShapeDtypeStruct(queries.shape, low),
+                jax.ShapeDtypeStruct(keys.shape, low),
+                jax.ShapeDtypeStruct(values.shape, low),
+            ),
+            in_specs=[hbm] * 2,
+            out_specs=(hbm,) * 3,
+            scratch_shapes=[
+                pltpu.VMEM(queries.shape, low),
+                pltpu.VMEM((2, *keys.shape), low),
+                dma((pieces + 2,)),
+                dma((pieces + 2,)),
+            ],
+            compiler_params=pltpu.CompilerParams(vmem_limit_bytes=63 * 1024 * 1024),
+        )(dq, dkv)
 
     placed = P(("ctx", "head"), None)
     return jax.shard_map(

time: 61.2 us -> 57.4 us (0.938)
  local copies, waits for them, and re-layouts: 3.71 us -> 0 us
    unnamed x7 -> x0, local copies, waits for them, and re-layouts: 3.71 us -> none
    pallas_call x1, Pallas kernels: 56.7 us -> 54.5 us  [local(): pl.pallas_call(functools.partial(kernel, parts, devices, group), out_shap...]
    pallas_call x0 -> x1, Pallas kernels: none -> 2.09 us  [local(): pl.pallas_call(functools.partial(finish, pieces), out_shape=(jax.ShapeDty...]
where the time goes in v2:
time: 57.4 us; the launch traced here: 57.3 us
  Pallas kernels  56.6 us (99%)
  between operations  0.64 us (1%)
    pallas_call x1, Pallas kernels, local(): pl.pallas_call(functools.partial(kernel, parts, devices, group), out_shap...  54.5 us
    pallas_call x1, Pallas kernels, local(): pl.pallas_call(functools.partial(finish, pieces), out_shape=(jax.ShapeDty...  2.09 us

profile of v2, /device:TPU:1, one launch (start us, length us, event | category | flops | bytes accessed | tf_op | source)
XLA Modules:
  0.0 57.3 jit_solution(738685564411797075)
XLA Ops:
  0.6 54.5 %shard_map.85 = (bf16[64,6144]{1,0:T(8,128)(2,1)}, bf16[2,64,1024]{2,1,0:T(8,128)(2,1)}) custom-call(bf16[64,6144]{1,0:T(8,128)(2,1)} %q_hbm.1, bf16[64,1024]{1,0:T(8,128)(2,1)} %k_hbm.1, bf16[64,1024]{1,0:T(8,128)(2,1)} %v_hbm.1, bf16[64,6144]{1,0:T(8,128)(2,1)} %o_hbm.1, bf16[64,6144]{1,0:T(8,128)(2,1)} %g_hbm.1, s32[128]{0:T(128)} %first_ref.1), custom_call_target="tpu_custom_call" | custom-call | flops 4026531840 | bytes 8000000 | tf_op jit(solution)/shard_map/pallas_call | solution.py:493
  55.2 2.1 %shard_map.86 = (bf16[64,6144]{1,0:T(8,128)(2,1)}, bf16[64,1024]{1,0:T(8,128)(2,1)}, bf16[64,1024]{1,0:T(8,128)(2,1)}) custom-call(bf16[64,6144]{1,0:T(8,128)(2,1)} %get-tuple-element.5.dq, bf16[2,64,1024]{2,1,0:T(8,128)(2,1)} %get-tuple-element.6.dkv), custom_call_target="tpu_custom_call" | custom-call | tf_op jit(solution)/shard_map/pallas_call | solution.py:537

commit v3 on v2

--- a/solution.py
+++ b/solution.py
@@ -41,6 +41,10 @@
     k_band,
     v_band,
     k_turned,
+    scores_a,
+    scores_b,
+    grads_a,
+    grads_b,
     total,
     dq_out,
     terms,
@@ -73,6 +77,23 @@
     def other(off):
         return lax.rem(h + off, devices)
 
+    barrier = pltpu.get_barrier_semaphore()
+
+    def greet_row(off, carry):
+        pl.semaphore_signal(barrier, inc=1, device_id=(p, other(off)), device_id_type=MESH)
+        return carry
+
+    def greet_near(off, carry):
+        for shift in (1, -1):
+            pl.semaphore_signal(
+                barrier, inc=1, device_id=(at(shift), other(off)), device_id_type=MESH
+            )
+        return carry
+
+    lax.fori_loop(1, devices, greet_row, 0)
+    lax.fori_loop(0, devices, greet_near, 0)
+    for shift in (2, -2):
+        pl.semaphore_signal(barrier, inc=1, device_id=(at(shift), h), device_id_type=MESH)
     load_q = pltpu.make_async_copy(q_hbm, q_own, load_sem.at[0])
     load_g = pltpu.make_async_copy(g_hbm, g_own, load_sem.at[1])
     load_o = pltpu.make_async_copy(o_hbm, o_own, load_sem.at[2])
@@ -80,23 +101,6 @@
     load_g.start()
     load_o.start()
 
-    barrier = pltpu.get_barrier_semaphore()
-
-    def greet_row(off, carry):
-        pl.semaphore_signal(barrier, inc=1, device_id=(p, other(off)), device_id_type=MESH)
-        return carry
-
-    def greet_near(off, carry):
-        for shift in (1, -1):
-            pl.semaphore_signal(
-                barrier, inc=1, device_id=(at(shift), other(off)), device_id_type=MESH
-            )
-        return carry
-
-    lax.fori_loop(1, devices, greet_row, 0)
-    lax.fori_loop(0, devices, greet_near, 0)
-    for shift in (2, -2):
-        pl.semaphore_signal(barrier, inc=1, device_id=(at(shift), h), device_id_type=MESH)
     pl.semaphore_wait(barrier, 3 * devices + 1)
 
     def rows_at(start, count):
@@ -311,29 +315,17 @@
         lax.fori_loop(late * half, (late + 1) * half, send_part, 0)
 
     reach = WINDOW * BLOCK
+    held_scores, held_grads = (scores_a, scores_b), (grads_a, grads_b)
     lane = lax.broadcasted_iota(jnp.int32, (BLOCK, HEAD_DIM), 1)
 
-    def pair(k, carry):
-        late = ((k + 1) % 2) * (1 - k // 4) + (k // 4) * (k % 2)
-        i = 2 * (k // 2)
-
-        @pl.when(k == 1)
-        def _():
-            far[0].wait_recv()
-            far[1].wait_recv()
-            turn(0)
-
-        @pl.when(k == 2)
-        def _():
-            wait_heads(2, 2, 1)
-
-        @pl.when(k == 4)
-        def _():
-            wait_heads(4, 2, 2)
-
+    def operands(late, i):
         query_rows = rows_at(late * BLOCK, BLOCK)
         key_rows = rows_at(late * BLOCK, reach)
         heads = [lanes_at((i + n) * HEAD_DIM, HEAD_DIM) for n in range(2)]
+        return query_rows, key_rows, heads
+
+    def products(slot, late, i):
+        query_rows, key_rows, heads = operands(late, i)
         q = jnp.concatenate([qg[0, query_rows, cols] for cols in heads], axis=0)
         g = jnp.concatenate([qg[1, query_rows, cols] for cols in heads], axis=0)
         corr = corr_cols[query_rows, :].astype(jnp.float32)
@@ -344,8 +336,17 @@
             ],
             axis=0,
         )
-        score = contract_last(k_band[key_rows, :], q)
-        grads = contract_last(v_band[key_rows, :], jnp.concatenate([g, corr], axis=1))
+        held_scores[slot][...] = contract_last(k_band[key_rows, :], q)
+        held_grads[slot][...] = contract_last(
+            v_band[key_rows, :], jnp.concatenate([g, corr], axis=1)
+        )
+
+    def returns(slot, late, i):
+        query_rows, key_rows, heads = operands(late, i)
+        q = jnp.concatenate([qg[0, query_rows, cols] for cols in heads], axis=0)
+        g = jnp.concatenate([qg[1, query_rows, cols] for cols in heads], axis=0)
+        score = held_scores[slot][...]
+        grads = held_grads[slot][...]
         first = first_ref[2 * p + late]
         tiles = [score[t * BLOCK : (t + 1) * BLOCK] for t in range(WINDOW)]
         biases = [
@@ -376,24 +377,29 @@
         for n in range(2):
             dq_out[query_rows, heads[n]] = dq[n * BLOCK : (n + 1) * BLOCK]
 
-        @pl.when(k == 1)
-        def _():
-            send_dq(0, 2)
-
-        @pl.when(k == 3)
-        def _():
-            send_dq(2, 2)
-
-        @pl.when(k == 4)
-        def _():
-            round_terms(0, half)
-            pass_back.start()
-            send_half(4, 2, 0)
-
-        return carry
-
     wait_heads(0, 2, 0)
-    lax.fori_loop(0, group, pair, 0)
+    products(0, 1, 0)
+    returns(0, 1, 0)
+    far[0].wait_recv()
+    far[1].wait_recv()
+    turn(0)
+    products(1, 0, 0)
+    wait_heads(2, 2, 1)
+    products(0, 1, 2)
+    returns(1, 0, 0)
+    products(1, 0, 2)
+    returns(0, 1, 2)
+    send_dq(0, 2)
+    returns(1, 0, 2)
+    send_dq(2, 2)
+    wait_heads(4, 2, 2)
+    products(0, 0, 4)
+    products(1, 1, 4)
+    returns(0, 0, 4)
+    round_terms(0, half)
+    pass_back.start()
+    send_half(4, 2, 0)
+    returns(1, 1, 4)
 
     round_terms(half, devices)
 
@@ -509,6 +515,10 @@
                 pltpu.VMEM((band, HEAD_DIM), low),
                 pltpu.VMEM((band, 2 * HEAD_DIM), low),
                 pltpu.VMEM((HEAD_DIM, band), low),
+                pltpu.VMEM((WINDOW * BLOCK, 2 * BLOCK), full),
+                pltpu.VMEM((WINDOW * BLOCK, 2 * BLOCK), full),
+                pltpu.VMEM((WINDOW * BLOCK, 2 * BLOCK), full),
+                pltpu.VMEM((WINDOW * BLOCK, 2 * BLOCK), full),
                 pltpu.VMEM((2, band, HEAD_DIM), full),
                 pltpu.VMEM((2 * BLOCK, width), low),
                 pltpu.VMEM((band // rows, 2, rows, HEAD_DIM), low),

time: 57.4 us -> 58.3 us (1.016)
  Pallas kernels: 56.6 us -> 57.5 us
    pallas_call x1, Pallas kernels: 54.5 us -> 55.4 us  [local(): pl.pallas_call(functools.partial(kernel, parts, devices, group), out_shap...]
where the time goes in v3:
time: 58.3 us; the launch traced here: 58.1 us
  Pallas kernels  57.5 us (99%)
  between operations  0.64 us (1%)
    pallas_call x1, Pallas kernels, local(): pl.pallas_call(functools.partial(kernel, parts, devices, group), out_shap...  55.4 us
    pallas_call x1, Pallas kernels, local(): pl.pallas_call(functools.partial(finish, pieces), out_shape=(jax.ShapeDty...  2.09 us

profile of v3, /device:TPU:1, one launch (start us, length us, event | category | flops | bytes accessed | tf_op | source)
XLA Modules:
  0.0 58.1 jit_solution(15131368123693051500)
XLA Ops:
  0.6 55.4 %shard_map.85 = (bf16[64,6144]{1,0:T(8,128)(2,1)}, bf16[2,64,1024]{2,1,0:T(8,128)(2,1)}) custom-call(bf16[64,6144]{1,0:T(8,128)(2,1)} %q_hbm.1, bf16[64,1024]{1,0:T(8,128)(2,1)} %k_hbm.1, bf16[64,1024]{1,0:T(8,128)(2,1)} %v_hbm.1, bf16[64,6144]{1,0:T(8,128)(2,1)} %o_hbm.1, bf16[64,6144]{1,0:T(8,128)(2,1)} %g_hbm.1, s32[128]{0:T(128)} %first_ref.1), custom_call_target="tpu_custom_call" | custom-call | flops 4026531840 | bytes 8000000 | tf_op jit(solution)/shard_map/pallas_call | solution.py:499
  56.0 2.1 %shard_map.86 = (bf16[64,6144]{1,0:T(8,128)(2,1)}, bf16[64,1024]{1,0:T(8,128)(2,1)}, bf16[64,1024]{1,0:T(8,128)(2,1)}) custom-call(bf16[64,6144]{1,0:T(8,128)(2,1)} %get-tuple-element.5.dq, bf16[2,64,1024]{2,1,0:T(8,128)(2,1)} %get-tuple-element.6.dkv), custom_call_target="tpu_custom_call" | custom-call | tf_op jit(solution)/shard_map/pallas_call | solution.py:547

commit v4 on v2

--- a/solution.py
+++ b/solution.py
@@ -73,6 +73,33 @@
     def other(off):
         return lax.rem(h + off, devices)
 
+    barrier = pltpu.get_barrier_semaphore()
+
+    def greet_row(off, carry):
+        pl.semaphore_signal(barrier, inc=1, device_id=(p, other(off)), device_id_type=MESH)
+        return carry
+
+    lax.fori_loop(1, devices, greet_row, 0)
+    has_earlier, has_later = p >= 1, p <= parts - 2
+    has_second_earlier, has_second_later = p >= 2, p <= parts - 3
+    for shift, exists in ((1, has_later), (-1, has_earlier)):
+
+        @pl.when(exists)
+        def _():
+            def greet_near(off, carry):
+                pl.semaphore_signal(
+                    barrier, inc=1, device_id=(at(shift), other(off)), device_id_type=MESH
+                )
+                return carry
+
+            lax.fori_loop(0, devices, greet_near, 0)
+
+    for shift, exists in ((2, has_second_later), (-2, has_second_earlier)):
+
+        @pl.when(exists)
+        def _():
+            pl.semaphore_signal(barrier, inc=1, device_id=(at(shift), h), device_id_type=MESH)
+
     load_q = pltpu.make_async_copy(q_hbm, q_own, load_sem.at[0])
     load_g = pltpu.make_async_copy(g_hbm, g_own, load_sem.at[1])
     load_o = pltpu.make_async_copy(o_hbm, o_own, load_sem.at[2])
@@ -80,24 +107,28 @@
     load_g.start()
     load_o.start()
 
-    barrier = pltpu.get_barrier_semaphore()
-
-    def greet_row(off, carry):
-        pl.semaphore_signal(barrier, inc=1, device_id=(p, other(off)), device_id_type=MESH)
-        return carry
-
-    def greet_near(off, carry):
-        for shift in (1, -1):
-            pl.semaphore_signal(
-                barrier, inc=1, device_id=(at(shift), other(off)), device_id_type=MESH
-            )
-        return carry
-
-    lax.fori_loop(1, devices, greet_row, 0)
-    lax.fori_loop(0, devices, greet_near, 0)
-    for shift in (2, -2):
-        pl.semaphore_signal(barrier, inc=1, device_id=(at(shift), h), device_id_type=MESH)
-    pl.semaphore_wait(barrier, 3 * devices + 1)
+    @pl.when(p == 0)
+    def _():
+        k_band[BLOCK:own] = jnp.zeros((2 * BLOCK, HEAD_DIM), jnp.bfloat16)
+        v_band[BLOCK:own, 0:HEAD_DIM] = jnp.zeros((2 * BLOCK, HEAD_DIM), jnp.bfloat16)
+
+    @pl.when(p <= 1)
+    def _():
+        k_band[0:BLOCK] = jnp.zeros((BLOCK, HEAD_DIM), jnp.bfloat16)
+        v_band[0:BLOCK, 0:HEAD_DIM] = jnp.zeros((BLOCK, HEAD_DIM), jnp.bfloat16)
+
+    @pl.when(p == parts - 1)
+    def _():
+        arrived[1] = jnp.zeros((devices, 2, rows, HEAD_DIM), jnp.bfloat16)
+
+    @pl.when(p >= parts - 2)
+    def _():
+        far_terms[...] = jnp.zeros((half, 2, rows, HEAD_DIM), jnp.bfloat16)
+
+    after = parts - 1 - p
+    neighbours = (p + parts - 1) // parts + (after + parts - 1) // parts
+    seconds = (p + parts - 2) // parts + (after + parts - 2) // parts
+    pl.semaphore_wait(barrier, devices - 1 + devices * neighbours + seconds)
 
     def rows_at(start, count):
         return pl.ds(pl.multiple_of(start, 64), count)
@@ -205,7 +236,7 @@
                 device_id_type=MESH,
             )
         )
-        near[index].start()
+        pl.when(has_later)(near[index].start)
         far.append(
             pltpu.make_async_remote_copy(
                 src_ref=band.at[2 * BLOCK : 3 * BLOCK, 0:HEAD_DIM],
@@ -224,8 +255,8 @@
 
     turn(3)
     turn(4)
-    near[0].wait_recv()
-    far[0].start()
+    pl.when(has_earlier)(near[0].wait_recv)
+    pl.when(has_earlier & has_later)(far[0].start)
     turn(1)
     turn(2)
 
@@ -235,8 +266,8 @@
         square = jnp.concatenate([piece, jnp.zeros((112, HEAD_DIM), jnp.float32)], axis=0).T
         corr_cols[d * rows : (d + 1) * rows] = square[0:rows].astype(jnp.bfloat16)
 
-    near[1].wait_recv()
-    far[1].start()
+    pl.when(has_earlier)(near[1].wait_recv)
+    pl.when(has_earlier & has_later)(far[1].start)
     send_heads(4, 2, 2)
 
 
@@ -250,7 +281,7 @@
         return pltpu.make_async_remote_copy(
             src_ref=terms.at[r],
             dst_ref=arrived.at[distance, h],
-            send_sem=send_sem.at[6],
+            send_sem=send_sem.at[6 + 2 * distance],
             recv_sem=term_sem.at[distance],
             device_id=(at(-distance), d),
             device_id_type=MESH,
@@ -319,8 +350,8 @@
 
         @pl.when(k == 1)
         def _():
-            far[0].wait_recv()
-            far[1].wait_recv()
+            pl.when(has_second_earlier)(far[0].wait_recv)
+            pl.when(has_second_earlier)(far[1].wait_recv)
             turn(0)
 
         @pl.when(k == 2)
@@ -387,7 +418,7 @@
         @pl.when(k == 4)
         def _():
             round_terms(0, half)
-            pass_back.start()
+            pl.when(has_second_earlier)(pass_back.start)
             send_half(4, 2, 0)
 
         return carry
@@ -402,7 +433,10 @@
         term_copy(half + d, 1, d).start()
         return carry
 
-    lax.fori_loop(0, devices, send_near, 0)
+    @pl.when(has_earlier)
+    def _():
+        lax.fori_loop(0, devices, send_near, 0)
+
     send_half(4, 2, 1)
     def send_own(d, carry):
         source = terms.at[half + devices + d]
@@ -419,7 +453,7 @@
 
     round_terms(half + devices, half)
     lax.fori_loop(0, half, send_own, 0)
-    pass_back.wait_recv()
+    pl.when(has_second_later)(pass_back.wait_recv)
     for r in range(half):
         at_row = half + devices + half + r
         part = slice(at_row * rows, (at_row + 1) * rows)
@@ -432,7 +466,9 @@
     lax.fori_loop(half, devices, send_own, 0)
 
     pltpu.make_async_copy(arrived.at[0], arrived.at[0], term_sem.at[0]).wait()
-    pltpu.make_async_copy(arrived.at[1], arrived.at[1], term_sem.at[1]).wait()
+    pl.when(has_later)(
+        pltpu.make_async_copy(arrived.at[1], arrived.at[1], term_sem.at[1]).wait
+    )
     for d in range(devices):
         cols = slice(d * HEAD_DIM, (d + 1) * HEAD_DIM)
         for index in range(2):
@@ -449,11 +485,22 @@
     left(k_band.at[0 : 2 * most], 0)
     left(corr_in.at[0 : devices - 1], 1)
     left(qg.at[:, 0:most], 2)
-    left(k_band.at[0 : 2 * span], 3)
-    left(k_band.at[0 : 2 * BLOCK], 4)
-    pass_back.wait_send()
     left(dq_out.at[0:most], 5)
-    left(terms.at[0 : 2 * devices - 1], 6)
+    left(terms.at[0 : devices - 1], 6)
+
+    @pl.when(has_later)
+    def _():
+        left(k_band.at[0 : 2 * span], 3)
+
+    @pl.when(has_earlier & has_later)
+    def _():
+        left(k_band.at[0 : 2 * BLOCK], 4)
+
+    @pl.when(has_earlier)
+    def _():
+        left(terms.at[0:devices], 8)
+
+    pl.when(has_second_earlier)(pass_back.wait_send)
 
 
 def finish(pieces, dq, dkv, dq_hbm, dk_hbm, dv_hbm, held, held_kv, in_sem, out_sem):
@@ -523,7 +570,7 @@
                 dma,
                 dma((2,)),
                 dma,
-                dma((8,)),
+                dma((9,)),
             ],
             compiler_params=pltpu.CompilerParams(
                 collective_id=0,

time: 57.4 us -> 55.5 us (0.967)
  Pallas kernels: 56.6 us -> 54.5 us
    pallas_call x1, Pallas kernels: 54.5 us -> 52.4 us  [local(): pl.pallas_call(functools.partial(kernel, parts, devices, group), out_shap...]
where the time goes in v4:
time: 55.5 us; the launch traced here: 55.1 us
  Pallas kernels  54.5 us (98%)
  between operations  0.64 us (1%)
    pallas_call x1, Pallas kernels, local(): pl.pallas_call(functools.partial(kernel, parts, devices, group), out_shap...  52.4 us
    pallas_call x1, Pallas kernels, local(): pl.pallas_call(functools.partial(finish, pieces), out_shape=(jax.ShapeDty...  2.09 us

profile of v4, /device:TPU:1, one launch (start us, length us, event | category | flops | bytes accessed | tf_op | source)
XLA Modules:
  0.0 55.1 jit_solution(7655108044488784863)
XLA Ops:
  0.6 52.4 %shard_map.85 = (bf16[64,6144]{1,0:T(8,128)(2,1)}, bf16[2,64,1024]{2,1,0:T(8,128)(2,1)}) custom-call(bf16[64,6144]{1,0:T(8,128)(2,1)} %q_hbm.1, bf16[64,1024]{1,0:T(8,128)(2,1)} %k_hbm.1, bf16[64,1024]{1,0:T(8,128)(2,1)} %v_hbm.1, bf16[64,6144]{1,0:T(8,128)(2,1)} %o_hbm.1, bf16[64,6144]{1,0:T(8,128)(2,1)} %g_hbm.1, s32[128]{0:T(128)} %first_ref.1), custom_call_target="tpu_custom_call" | custom-call | flops 4026531840 | bytes 8000000 | tf_op jit(solution)/shard_map/pallas_call | solution.py:540
  53.1 2.1 %shard_map.86 = (bf16[64,6144]{1,0:T(8,128)(2,1)}, bf16[64,1024]{1,0:T(8,128)(2,1)}, bf16[64,1024]{1,0:T(8,128)(2,1)}) custom-call(bf16[64,6144]{1,0:T(8,128)(2,1)} %get-tuple-element.5.dq, bf16[2,64,1024]{2,1,0:T(8,128)(2,1)} %get-tuple-element.6.dkv), custom_call_target="tpu_custom_call" | custom-call | tf_op jit(solution)/shard_map/pallas_call | solution.py:584

commit v5 on v4

--- a/solution.py
+++ b/solution.py
@@ -81,7 +81,7 @@
 
     lax.fori_loop(1, devices, greet_row, 0)
     has_earlier, has_later = p >= 1, p <= parts - 2
-    has_second_earlier, has_second_later = p >= 2, p <= parts - 3
+    has_second_earlier = p >= 2
     for shift, exists in ((1, has_later), (-1, has_earlier)):
 
         @pl.when(exists)
@@ -94,12 +94,6 @@
 
             lax.fori_loop(0, devices, greet_near, 0)
 
-    for shift, exists in ((2, has_second_later), (-2, has_second_earlier)):
-
-        @pl.when(exists)
-        def _():
-            pl.semaphore_signal(barrier, inc=1, device_id=(at(shift), h), device_id_type=MESH)
-
     load_q = pltpu.make_async_copy(q_hbm, q_own, load_sem.at[0])
     load_g = pltpu.make_async_copy(g_hbm, g_own, load_sem.at[1])
     load_o = pltpu.make_async_copy(o_hbm, o_own, load_sem.at[2])
@@ -121,14 +115,13 @@
     def _():
         arrived[1] = jnp.zeros((devices, 2, rows, HEAD_DIM), jnp.bfloat16)
 
-    @pl.when(p >= parts - 2)
+    @pl.when((p == 0) | (p == parts - 1))
     def _():
         far_terms[...] = jnp.zeros((half, 2, rows, HEAD_DIM), jnp.bfloat16)
 
     after = parts - 1 - p
     neighbours = (p + parts - 1) // parts + (after + parts - 1) // parts
-    seconds = (p + parts - 2) // parts + (after + parts - 2) // parts
-    pl.semaphore_wait(barrier, devices - 1 + devices * neighbours + seconds)
+    pl.semaphore_wait(barrier, devices - 1 + devices * neighbours)
 
     def rows_at(start, count):
         return pl.ds(pl.multiple_of(start, 64), count)
@@ -292,7 +285,7 @@
         dst_ref=far_terms,
         send_sem=send_sem.at[7],
         recv_sem=far_term_sem,
-        device_id=(at(-2), h),
+        device_id=(at(-1), h),
         device_id_type=MESH,
     )
 
@@ -426,36 +419,31 @@
     wait_heads(0, 2, 0)
     lax.fori_loop(0, group, pair, 0)
 
-    round_terms(half, devices)
-
-    def send_near(off, carry):
-        d = other(off)
+    def send_near(d, carry):
         term_copy(half + d, 1, d).start()
         return carry
 
+    def send_own(off, carry):
+        d = other(off)
+        term_copy(half + devices + d, 0, d).start()
+        return carry
+
+    round_terms(half, half)
+
     @pl.when(has_earlier)
     def _():
-        lax.fori_loop(0, devices, send_near, 0)
-
+        lax.fori_loop(0, half, send_near, 0)
+
+    round_terms(half + devices, devices)
+    lax.fori_loop(1, devices, send_own, 0)
+    pltpu.make_async_copy(
+        terms.at[half + devices + h], arrived.at[0, h], term_sem.at[0]
+    ).start()
     send_half(4, 2, 1)
-    def send_own(d, carry):
-        source = terms.at[half + devices + d]
-
-        @pl.when(d != h)
-        def _():
-            term_copy(half + devices + d, 0, d).start()
-
-        @pl.when(d == h)
-        def _():
-            pltpu.make_async_copy(source, arrived.at[0, h], term_sem.at[0]).start()
-
-        return carry
-
-    round_terms(half + devices, half)
-    lax.fori_loop(0, half, send_own, 0)
-    pl.when(has_second_later)(pass_back.wait_recv)
+
+    pl.when(has_earlier & has_later)(pass_back.wait_recv)
     for r in range(half):
-        at_row = half + devices + half + r
+        at_row = devices + r
         part = slice(at_row * rows, (at_row + 1) * rows)
         terms[at_row, 0] = (
             total[0, part] * scaling + far_terms[r, 0].astype(jnp.float32)
@@ -463,7 +451,10 @@
         terms[at_row, 1] = (total[1, part] + far_terms[r, 1].astype(jnp.float32)).astype(
             jnp.bfloat16
         )
-    lax.fori_loop(half, devices, send_own, 0)
+
+    @pl.when(has_earlier)
+    def _():
+        lax.fori_loop(half, devices, send_near, 0)
 
     pltpu.make_async_copy(arrived.at[0], arrived.at[0], term_sem.at[0]).wait()
     pl.when(has_later)(

time: 55.5 us -> 54.6 us (0.984)
  the two profiles are of different devices: /device:TPU:1 before, /device:TPU:47 now
where the time goes in v5:
time: 54.6 us; the launch traced here: 54.5 us
  Pallas kernels  53.8 us (99%)
  between operations  0.64 us (1%)
    pallas_call x1, Pallas kernels, local(): pl.pallas_call(functools.partial(kernel, parts, devices, group), out_shap...  51.7 us
    pallas_call x1, Pallas kernels, local(): pl.pallas_call(functools.partial(finish, pieces), out_shape=(jax.ShapeDty...  2.09 us

profile of v5, /device:TPU:47, one launch (start us, length us, event | category | flops | bytes accessed | tf_op | source)
XLA Modules:
  0.0 54.5 jit_solution(4252798552444010002)
XLA Ops:
  0.6 51.7 %shard_map.85 = (bf16[64,6144]{1,0:T(8,128)(2,1)}, bf16[2,64,1024]{2,1,0:T(8,128)(2,1)}) custom-call(bf16[64,6144]{1,0:T(8,128)(2,1)} %q_hbm.1, bf16[64,1024]{1,0:T(8,128)(2,1)} %k_hbm.1, bf16[64,1024]{1,0:T(8,128)(2,1)} %v_hbm.1, bf16[64,6144]{1,0:T(8,128)(2,1)} %o_hbm.1, bf16[64,6144]{1,0:T(8,128)(2,1)} %g_hbm.1, s32[128]{0:T(128)} %first_ref.1), custom_call_target="tpu_custom_call" | custom-call | flops 4026531840 | bytes 8000000 | tf_op jit(solution)/shard_map/pallas_call | solution.py:531
  52.4 2.1 %shard_map.86 = (bf16[64,6144]{1,0:T(8,128)(2,1)}, bf16[64,1024]{1,0:T(8,128)(2,1)}, bf16[64,1024]{1,0:T(8,128)(2,1)}) custom-call(bf16[64,6144]{1,0:T(8,128)(2,1)} %get-tuple-element.5.dq, bf16[2,64,1024]{2,1,0:T(8,128)(2,1)} %get-tuple-element.6.dkv), custom_call_target="tpu_custom_call" | custom-call | tf_op jit(solution)/shard_map/pallas_call | solution.py:575

commit v6 on v5

--- a/solution.py
+++ b/solution.py
@@ -41,6 +41,10 @@
     k_band,
     v_band,
     k_turned,
+    scores_a,
+    scores_b,
+    grads_a,
+    grads_b,
     total,
     dq_out,
     terms,
@@ -335,29 +339,17 @@
         lax.fori_loop(late * half, (late + 1) * half, send_part, 0)
 
     reach = WINDOW * BLOCK
+    held_scores, held_grads = (scores_a, scores_b), (grads_a, grads_b)
     lane = lax.broadcasted_iota(jnp.int32, (BLOCK, HEAD_DIM), 1)
 
-    def pair(k, carry):
-        late = ((k + 1) % 2) * (1 - k // 4) + (k // 4) * (k % 2)
-        i = 2 * (k // 2)
-
-        @pl.when(k == 1)
-        def _():
-            pl.when(has_second_earlier)(far[0].wait_recv)
-            pl.when(has_second_earlier)(far[1].wait_recv)
-            turn(0)
-
-        @pl.when(k == 2)
-        def _():
-            wait_heads(2, 2, 1)
-
-        @pl.when(k == 4)
-        def _():
-            wait_heads(4, 2, 2)
-
+    def operands(late, i):
         query_rows = rows_at(late * BLOCK, BLOCK)
         key_rows = rows_at(late * BLOCK, reach)
         heads = [lanes_at((i + n) * HEAD_DIM, HEAD_DIM) for n in range(2)]
+        return query_rows, key_rows, heads
+
+    def products(slot, late, i):
+        query_rows, key_rows, heads = operands(late, i)
         q = jnp.concatenate([qg[0, query_rows, cols] for cols in heads], axis=0)
         g = jnp.concatenate([qg[1, query_rows, cols] for cols in heads], axis=0)
         corr = corr_cols[query_rows, :].astype(jnp.float32)
@@ -368,8 +360,17 @@
             ],
             axis=0,
         )
-        score = contract_last(k_band[key_rows, :], q)
-        grads = contract_last(v_band[key_rows, :], jnp.concatenate([g, corr], axis=1))
+        held_scores[slot][...] = contract_last(k_band[key_rows, :], q)
+        held_grads[slot][...] = contract_last(
+            v_band[key_rows, :], jnp.concatenate([g, corr], axis=1)
+        )
+
+    def returns(slot, late, i):
+        query_rows, key_rows, heads = operands(late, i)
+        q = jnp.concatenate([qg[0, query_rows, cols] for cols in heads], axis=0)
+        g = jnp.concatenate([qg[1, query_rows, cols] for cols in heads], axis=0)
+        score = held_scores[slot][...]
+        grads = held_grads[slot][...]
         first = first_ref[2 * p + late]
         tiles = [score[t * BLOCK : (t + 1) * BLOCK] for t in range(WINDOW)]
         biases = [
@@ -400,24 +401,29 @@
         for n in range(2):
             dq_out[query_rows, heads[n]] = dq[n * BLOCK : (n + 1) * BLOCK]
 
-        @pl.when(k == 1)
-        def _():
-            send_dq(0, 2)
-
-        @pl.when(k == 3)
-        def _():
-            send_dq(2, 2)
-
-        @pl.when(k == 4)
-        def _():
-            round_terms(0, half)
-            pl.when(has_second_earlier)(pass_back.start)
-            send_half(4, 2, 0)
-
-        return carry
-
     wait_heads(0, 2, 0)
-    lax.fori_loop(0, group, pair, 0)
+    products(0, 1, 0)
+    returns(0, 1, 0)
+    pl.when(has_second_earlier)(far[0].wait_recv)
+    pl.when(has_second_earlier)(far[1].wait_recv)
+    turn(0)
+    products(1, 0, 0)
+    wait_heads(2, 2, 1)
+    products(0, 1, 2)
+    returns(1, 0, 0)
+    products(1, 0, 2)
+    send_dq(0, 2)
+    returns(0, 1, 2)
+    returns(1, 0, 2)
+    send_dq(2, 2)
+    wait_heads(4, 2, 2)
+    products(0, 0, 4)
+    products(1, 1, 4)
+    returns(0, 0, 4)
+    round_terms(0, half)
+    pl.when(has_second_earlier)(pass_back.start)
+    send_half(4, 2, 0)
+    returns(1, 1, 4)
 
     def send_near(d, carry):
         term_copy(half + d, 1, d).start()
@@ -547,6 +553,10 @@
                 pltpu.VMEM((band, HEAD_DIM), low),
                 pltpu.VMEM((band, 2 * HEAD_DIM), low),
                 pltpu.VMEM((HEAD_DIM, band), low),
+                pltpu.VMEM((WINDOW * BLOCK, 2 * BLOCK), full),
+                pltpu.VMEM((WINDOW * BLOCK, 2 * BLOCK), full),
+                pltpu.VMEM((WINDOW * BLOCK, 2 * BLOCK), full),
+                pltpu.VMEM((WINDOW * BLOCK, 2 * BLOCK), full),
                 pltpu.VMEM((2, band, HEAD_DIM), full),
                 pltpu.VMEM((2 * BLOCK, width), low),
                 pltpu.VMEM((band // rows, 2, rows, HEAD_DIM), low),

time: 54.6 us -> 54.4 us (level)
  the two profiles are of different devices: /device:TPU:47 before, /device:TPU:41 now
where the time goes in v6:
time: 54.4 us; the launch traced here: 54.2 us
  Pallas kernels  53.6 us (99%)
  between operations  0.64 us (1%)
    pallas_call x1, Pallas kernels, local(): pl.pallas_call(functools.partial(kernel, parts, devices, group), out_shap...  51.5 us
    pallas_call x1, Pallas kernels, local(): pl.pallas_call(functools.partial(finish, pieces), out_shape=(jax.ShapeDty...  2.09 us

profile of v6, /device:TPU:41, one launch (start us, length us, event | category | flops | bytes accessed | tf_op | source)
XLA Modules:
  0.0 54.2 jit_solution(12644045367705621682)
XLA Ops:
  0.6 51.5 %shard_map.85 = (bf16[64,6144]{1,0:T(8,128)(2,1)}, bf16[2,64,1024]{2,1,0:T(8,128)(2,1)}) custom-call(bf16[64,6144]{1,0:T(8,128)(2,1)} %q_hbm.1, bf16[64,1024]{1,0:T(8,128)(2,1)} %k_hbm.1, bf16[64,1024]{1,0:T(8,128)(2,1)} %v_hbm.1, bf16[64,6144]{1,0:T(8,128)(2,1)} %o_hbm.1, bf16[64,6144]{1,0:T(8,128)(2,1)} %g_hbm.1, s32[128]{0:T(128)} %first_ref.1), custom_call_target="tpu_custom_call" | custom-call | flops 4026531840 | bytes 8000000 | tf_op jit(solution)/shard_map/pallas_call | solution.py:537
  52.1 2.1 %shard_map.86 = (bf16[64,6144]{1,0:T(8,128)(2,1)}, bf16[64,1024]{1,0:T(8,128)(2,1)}, bf16[64,1024]{1,0:T(8,128)(2,1)}) custom-call(bf16[64,6144]{1,0:T(8,128)(2,1)} %get-tuple-element.5.dq, bf16[2,64,1024]{2,1,0:T(8,128)(2,1)} %get-tuple-element.6.dkv), custom_call_target="tpu_custom_call" | custom-call | tf_op jit(solution)/shard_map/pallas_call | solution.py:585
